TPU v7x, 32 devices: a whole 2x2x4 slice. The times are simulated.
32 devices in a mesh: dp: 16 (over z, y, x), mp: 2 (over core).
Axes of the slice: x: 2, y: 2, z: 4, core: 2. Of those that a mesh axis runs over, the one named last changes fastest.
Arguments:
- store_rows: bfloat16 [4096, 8192], P('dp', 'mp'), may hold values from -6 to 6
- source_shard: int32 [512], replicated, may hold values from 0 to 15, as said below
- source_row: int32 [512], replicated, may hold values from 0 to 255
- state_len: int32 [16], replicated, may hold values from 1 to 64, 512 in all
- visits: int32 [16], replicated, may hold values from 1 to 4095
- gain: bfloat16 [8192], P('mp'), may hold values from 0.5 to 1.5
- w_gate: bfloat16 [8192, 22016], P('mp', 'dp'), may hold values from -0.0625 to 0.0625
- w_up: bfloat16 [8192, 22016], P('mp', 'dp'), may hold values from -0.0625 to 0.0625
- w_down: bfloat16 [22016, 8192], P('dp', 'mp'), may hold values from -0.0390625 to 0.0390625
- upstream: bfloat16 [512, 8192], P(None, 'mp'), may hold values from -0.52734375 to 0.52734375
Outputs:
- layer_out: bfloat16 [512, 8192], P('dp', 'mp')
- grad_gate: bfloat16 [8192, 22016], P('mp', 'dp')
- grad_up: bfloat16 [8192, 22016], P('mp', 'dp')
- grad_down: bfloat16 [22016, 8192], P('dp', 'mp')
Inputs may be any that keep to these rules, and one draw needn't show every extreme that they name: `source_shard`: block b holds training rows b * 32 to (b + 1) * 32 - 1. No shard is named more than 4 times in one block nor more than 64 times in all; one shard, drawn from the seed, is named exactly 4 times in every block. `state_len`: the lengths sum to 512.
All inputs are finite; a program needn't handle non-finite values.
Results may differ from a plain program's by a relative error of at most 0.017.
Values may be sent and summed in bfloat16 or wider, within the bound.
A program may use at most 192 MiB of HBM per device.

v0:
```python
import jax
import jax.numpy as jnp
from jax import lax
from jax.sharding import PartitionSpec as P

D = 8192


epsilon = 1e-05


def pick_rows(store_rows, source_row, target, row_ids, slots):
    picked = jnp.zeros((slots,), jnp.int32).at[target].set(row_ids, mode="drop")
    filled = jnp.zeros((slots,), jnp.bool_).at[target].set(True, mode="drop")
    chosen = store_rows[source_row[picked]]
    return jnp.where(filled[:, None], chosen, jnp.zeros_like(chosen))


def shards(
    store_rows, source_shard, source_row, state_len, visits, gain, w_gate, w_up, w_down, upstream
):
    count_dp = lax.axis_size("dp")
    count_mp = lax.axis_size("mp")
    index_dp = lax.axis_index("dp")
    index_mp = lax.axis_index("mp")
    total_rows = source_shard.shape[0]
    block_rows = total_rows // count_dp
    share_rows = total_rows // count_mp
    hidden_part = w_gate.shape[1]
    pair_cap = max(block_rows // 8, 1)
    shard_cap = count_dp * pair_cap
    row_ids = jnp.arange(total_rows, dtype=jnp.int32)
    owned = source_shard == index_dp
    one_hot = (source_shard[:, None] == jnp.arange(count_dp, dtype=jnp.int32)[None, :]).astype(
        jnp.int32
    )
    before = jnp.cumsum(one_hot, axis=0) - one_hot
    shard_rank = jnp.sum(before * one_hot, axis=1)
    target = jnp.where(owned, shard_rank, shard_cap)
    outgoing = pick_rows(store_rows, source_row, target, row_ids, shard_cap)
    arrived = lax.all_gather(outgoing, "dp", axis=0, tiled=True)
    train_rows = arrived[source_shard * shard_cap + shard_rank]
    rows_float = train_rows.astype(jnp.float32)
    squares = jnp.sum(rows_float * rows_float, axis=1)
    scaled = (rows_float * gain.astype(jnp.float32)[None, :]).astype(jnp.bfloat16)
    share_first = index_mp * share_rows
    square_total = lax.psum(squares, "mp")
    inverse = lax.rsqrt(square_total / D + epsilon)
    block = scaled
    both_share = lax.psum_scatter(
        jnp.concatenate(
            [
                jnp.dot(block, w_gate, preferred_element_type=jnp.float32),
                jnp.dot(block, w_up, preferred_element_type=jnp.float32),
            ],
            axis=1,
        ),
        "mp",
        scatter_dimension=0,
        tiled=True,
    )
    inverse_share = lax.dynamic_slice_in_dim(inverse, share_first, share_rows, 0)
    gate_share = inverse_share[:, None] * both_share[:, :hidden_part]
    up_share = inverse_share[:, None] * both_share[:, hidden_part:]
    hidden_share = (jax.nn.silu(gate_share) * up_share).astype(jnp.bfloat16)
    hidden_all = lax.all_gather(hidden_share, "mp", axis=0, tiled=True)
    block = hidden_all
    down_block = lax.psum_scatter(
        jnp.dot(block, w_down, preferred_element_type=jnp.float32).astype(jnp.bfloat16),
        "dp",
        scatter_dimension=0,
        tiled=True,
    ).astype(jnp.float32)
    own_rows = lax.dynamic_slice_in_dim(rows_float, index_dp * block_rows, block_rows, 0)
    layer_out = (own_rows + down_block).astype(jnp.bfloat16)
    ends = jnp.cumsum(state_len)
    starts = ends - state_len
    member = ((row_ids[:, None] >= starts[None, :]) & (row_ids[:, None] < ends[None, :])).astype(
        jnp.float32
    )
    importance = jnp.log1p(visits.astype(jnp.float32))
    per_state = total_rows * importance / (state_len.astype(jnp.float32) * jnp.sum(importance))
    row_weight = jnp.sum(member * per_state[None, :], axis=1)
    out_grad = (upstream.astype(jnp.float32) * row_weight[:, None]).astype(jnp.bfloat16)
    grad_down = lax.dot_general(
        hidden_all, out_grad, (((0,), (0,)), ((), ())), preferred_element_type=jnp.float32
    ).astype(jnp.bfloat16)
    block = out_grad
    grad_hidden = lax.psum_scatter(
        lax.dot_general(
            block, w_down, (((1,), (1,)), ((), ())), preferred_element_type=jnp.float32
        ).astype(jnp.bfloat16),
        "mp",
        scatter_dimension=0,
        tiled=True,
    ).astype(jnp.float32)
    sigmoid_gate = jax.nn.sigmoid(gate_share)
    gate_delta = (
        inverse_share[:, None]
        * grad_hidden
        * up_share
        * sigmoid_gate
        * (1.0 + gate_share * (1.0 - sigmoid_gate))
    ).astype(jnp.bfloat16)
    up_delta = (inverse_share[:, None] * grad_hidden * gate_share * sigmoid_gate).astype(
        jnp.bfloat16
    )
    block = scaled
    gate_add = lax.dot_general(
        block,
        lax.all_gather(gate_delta, "mp", axis=0, tiled=True),
        (((0,), (0,)), ((), ())),
        preferred_element_type=jnp.float32,
    )
    up_add = lax.dot_general(
        block,
        lax.all_gather(up_delta, "mp", axis=0, tiled=True),
        (((0,), (0,)), ((), ())),
        preferred_element_type=jnp.float32,
    )
    return (layer_out, gate_add.astype(jnp.bfloat16), up_add.astype(jnp.bfloat16), grad_down)


def solution(mesh):
    in_specs = (
        P("dp", "mp"),
        P(),
        P(),
        P(),
        P(),
        P("mp"),
        P("mp", "dp"),
        P("mp", "dp"),
        P("dp", "mp"),
        P(None, "mp"),
    )
    out_specs = (P("dp", "mp"), P("mp", "dp"), P("mp", "dp"), P("dp", "mp"))
    return jax.shard_map(shards, mesh=mesh, in_specs=in_specs, out_specs=out_specs, check_vma=False)
```

profile of v0, /device:TPU:0, one launch (start us, length us, event | category | flops | bytes accessed | tf_op | source)
XLA Modules:
  0.0 316.3 jit_solution(4900569325766204781)
XLA Ops:
  8.1 0.8 fusion.5
  8.9 1.1 reduce-window.18
  10.3 0.8 fusion.4
  11.1 0.7 compare_select_fusion
  11.8 2.4 scatter_custom_fusion.1
  14.2 1.5 gather_fusion
  15.7 0.9 gather_fusion.1
  16.6 2.4 scatter_custom_fusion
  19.1 0.9 broadcast_select_fusion
  20.3 0.6 fusion.10
  20.9 0.7 multiply_divide_fusion
  21.7 12.3 %convolution_convert_fusion.4 = bf16[512,1376]{0,1:T(8,128)(2,1)} fusion(bf16[1376,4096]{1,0:T(8,128)(2,1)} %param.18, bf16[512,4096]{1,0:T(8,128)(2,1)} %param.19, f32[512]{0:T(512)S(1)} %select_reduce_fusion), kind=kOutput, calls=%fused_computation.13 | convolution fusion | flops 5778358272 | bytes 16877568 | tf_op jit(solution)/shard_map/dot_general | solution.py:90
  34.3 101.4 %all-gather.5.cloned.1.call-done = bf16[1024,4096]{1,0:T(8,128)(2,1)} async-done(((bf16[64,4096]{1,0:T(8,128)(2,1)}), bf16[1024,4096]{1,0:T(8,128)(2,1)}) %all-gather.5.cloned.1.call-update) | async-done | bytes 8388624 | tf_op jit(solution)/shard_map/all_gather | solution.py:41
  135.7 13.0 %gather_fusion.2 = bf16[512,4096]{1,0:T(8,128)(2,1)} fusion(bf16[1024,4096]{1,0:T(8,128)(2,1)} %all-gather.5.cloned.1.call-done, s32[1024]{0:T(1024)S(1)} %pad_clamp_fusion), kind=kCustom, calls=%fused_computation.2 | custom fusion | bytes 8390656 | tf_op jit(solution)/shard_map/gather | solution.py:42
  148.7 11.5 %fusion = f32[512,1376]{0,1:T(8,128)S(1)} fusion(bf16[4096,1376]{0,1:T(8,128)(2,1)} %param.17, f32[4096]{0:T(1024)S(1)} %convert_element_type.65, bf16[512,4096]{1,0:T(8,128)(2,1)} %gather_fusion.2), kind=kOutput, calls=%fused_computation.14 | convolution fusion | flops 5777653760 | bytes 18300928 | tf_op jit(solution)/shard_map/dot_general | solution.py:54
  160.3 8.9 %fusion.1 = f32[512,1376]{0,1:T(8,128)S(1)} fusion(bf16[4096,1376]{0,1:T(8,128)(2,1)} %param.16, f32[4096]{0:T(1024)S(1)} %convert_element_type.65, bf16[512,4096]{1,0:T(8,128)(2,1)S(1)} %copy-done.2), kind=kOutput, calls=%fused_computation.15 | convolution fusion | flops 5777653760 | bytes 18300928 | tf_op jit(solution)/shard_map/dot_general | solution.py:53
  169.1 3.1 pad_maximum_fusion
  172.3 3.1 multiply_reduce_fusion
  175.4 2.5 psum.7
  178.0 6.2 %reduce-scatter.4.cloned.1.call-done = f32[256,2752]{0,1:T(8,128)} async-done(((f32[512,2752]{0,1:T(8,128)}), f32[256,2752]{0,1:T(8,128)}) %reduce-scatter.4.cloned.1.call-update) | async-done | bytes 2818064 | tf_op jit(solution)/shard_map/reduce_scatter | solution.py:50
  184.2 4.1 %multiply_convert_fusion.8 = (bf16[256,1376]{0,1:T(8,128)(2,1)}, bf16[256,1376]{0,1:T(8,128)(2,1)}, bf16[256,1376]{0,1:T(8,128)(2,1)}) fusion(bf16[256,1376]{0,1:T(8,128)(2,1)} %reduce-scatter.8.cloned.1.call-done, f32[256,2752]{0,1:T(8,128)} %reduce-scatter.4.cloned.1.call-done, f32[256]{0:T(256)S(1)} %dynamic_slice.7), kind=kLoop, calls=%fused_computation.18 | loop fusion | flops 7045120 | bytes 5637120 | tf_op jit(solution)/shard_map/convert_element_type | solution.py:105
  188.4 0.7 all-gather.9.cloned.1.call-update
  189.2 0.7 all-gather.11.cloned.1.call-update
  189.9 0.3 reduce-scatter.6.cloned.1.call-start
  190.1 8.9 %all-gather.7.cloned.1.call-done = bf16[512,1376]{0,1:T(8,128)(2,1)} async-done(((bf16[256,1376]{0,1:T(8,128)(2,1)}), bf16[512,1376]{0,1:T(8,128)(2,1)}) %all-gather.7.cloned.1.call-update) | async-done | bytes 1409040 | tf_op jit(solution)/shard_map/all_gather | solution.py:66
  199.0 11.3 %convolution_convert_fusion.3 = bf16[512,4096]{1,0:T(8,128)(2,1)} fusion(bf16[512,1376]{0,1:T(8,128)(2,1)} %all-gather.7.cloned.1.call-done, bf16[1376,4096]{1,0:T(8,128)(2,1)} %param.18), kind=kOutput, calls=%fused_computation.11 | convolution fusion | flops 5773459456 | bytes 16875520 | tf_op jit(solution)/shard_map/dot_general | solution.py:69
  210.4 6.6 %convert_element_type.64 = f32[512,4096]{1,0:T(8,128)} convert(bf16[512,4096]{1,0:T(8,128)(2,1)} %gather_fusion.2) | non-fusion elementwise | flops 2097152 | bytes 12582912 | tf_op jit(solution)/shard_map/convert_element_type | solution.py:43
  217.0 8.9 %convolution_convert_fusion.2 = bf16[1376,4096]{1,0:T(8,128)(2,1)} fusion(bf16[512,1376]{0,1:T(8,128)(2,1)S(1)} %copy-done.7, bf16[512,4096]{1,0:T(8,128)(2,1)S(1)} %copy-done.6, f32[512]{0:T(512)S(1)} %select_reduce_fusion), kind=kOutput, calls=%fused_computation.7 | convolution fusion | flops 5783289856 | bytes 16877568 | tf_op jit(solution)/shard_map/dot_general | solution.py:85
  225.9 10.7 %convolution_convert_fusion.1 = bf16[4096,1376]{0,1:T(8,128)(2,1)} fusion(bf16[512,1376]{0,1:T(8,128)(2,1)} %all-gather.9.cloned.1.call-done, f32[4096]{0:T(1024)S(1)} %convert_element_type.65, bf16[512,4096]{1,0:T(8,128)(2,1)} %gather_fusion.2), kind=kOutput, calls=%fused_computation.6 | convolution fusion | flops 5783289856 | bytes 16891904 | tf_op jit(solution)/shard_map/dot_general | solution.py:109
  236.7 10.9 %convolution_convert_fusion = bf16[4096,1376]{0,1:T(8,128)(2,1)} fusion(bf16[512,1376]{0,1:T(8,128)(2,1)} %all-gather.11.cloned.1.call-done, f32[4096]{0:T(1024)S(1)} %convert_element_type.65, bf16[512,4096]{1,0:T(8,128)(2,1)} %gather_fusion.2), kind=kOutput, calls=%fused_computation.5 | convolution fusion | flops 5783289856 | bytes 16891904 | tf_op jit(solution)/shard_map/dot_general | solution.py:115
  247.5 59.3 %reduce-scatter.6.cloned.1.call-done = bf16[32,4096]{1,0:T(8,128)(2,1)} async-done(((bf16[512,4096]{1,0:T(8,128)(2,1)}), bf16[32,4096]{1,0:T(8,128)(2,1)}) %reduce-scatter.6.cloned.1.call-update) | async-done | bytes 262160 | tf_op jit(solution)/shard_map/reduce_scatter | solution.py:68
  306.9 1.9 add_convert_fusion
  (48 shorter events, 1.3 us)
Async XLA Ops:
  8.0 7.7 %copy-start = (bf16[256,4096]{1,0:T(8,128)(2,1)S(1)}, bf16[256,4096]{1,0:T(8,128)(2,1)}, u32[]{:S(2)}) copy-start(bf16[256,4096]{1,0:T(8,128)(2,1)} %param.10) | copy-start | bytes 6291460
  8.0 12.0 %copy-start.4 = (s32[16]{0:T(128)S(1)}, s32[16]{0:T(128)}, u32[]{:S(2)}) copy-start(s32[16]{0:T(128)} %param.13) | copy-start | bytes 196
  8.0 12.3 %copy-start.5 = (s32[16]{0:T(128)S(1)}, s32[16]{0:T(128)}, u32[]{:S(2)}) copy-start(s32[16]{0:T(128)} %param.14) | copy-start | bytes 196
  8.0 127.7 %all-gather.5.cloned.1.call-start = ((), (), s32[]{:S(2)}) async-start(), calls=%async_computation.3 | async-start | bytes 8912896 | tf_op jit(solution)/shard_map/all_gather | solution.py:41
  20.0 158.0 %reduce-scatter.8.cloned.1.call-start = ((), (), s32[]{:S(2)}) async-start(), calls=%async_computation.7 | async-start | bytes 2113536 | tf_op jit(solution)/shard_map/reduce_scatter | solution.py:89
  21.7 12.5 %copy-start.3 = (bf16[4096]{0:T(1024)(128)(2,1)S(1)}, bf16[4096]{0:T(1024)(128)(2,1)}, u32[]{:S(2)}) copy-start(bf16[4096]{0:T(1024)(128)(2,1)} %param.15) | copy-start | bytes 24580
  34.0 150.2 %reduce-scatter.4.cloned.1.call-start = ((), (), s32[]{:S(2)}) async-start(), calls=%async_computation.4 | async-start | bytes 8454144 | tf_op jit(solution)/shard_map/reduce_scatter | solution.py:50
  148.7 11.6 %copy-start.2 = (bf16[512,4096]{1,0:T(8,128)(2,1)S(1)}, bf16[512,4096]{1,0:T(8,128)(2,1)}, u32[]{:S(2)}) copy-start(bf16[512,4096]{1,0:T(8,128)(2,1)} %gather_fusion.2) | copy-start | bytes 12582916
  172.3 26.7 %all-gather.7.cloned.1.call-start = ((), (), s32[]{:S(2)}) async-start(), calls=%async_computation.5 | async-start | bytes 2113536 | tf_op jit(solution)/shard_map/all_gather | solution.py:66
  188.4 37.5 %all-gather.9.cloned.1.call-start = ((), (), s32[]{:S(2)}) async-start(), calls=%async_computation.8 | async-start | bytes 2113536 | tf_op jit(solution)/shard_map/all_gather | solution.py:111
  189.1 47.5 %all-gather.11.cloned.1.call-start = ((), (), s32[]{:S(2)}) async-start(), calls=%async_computation.9 | async-start | bytes 2113536 | tf_op jit(solution)/shard_map/all_gather | solution.py:117
  189.9 117.0 %reduce-scatter.6.cloned.1.call-start = ((), (), s32[]{:S(2)}) async-start(), calls=%async_computation.6 | async-start | bytes 4456448 | tf_op jit(solution)/shard_map/reduce_scatter | solution.py:68
  210.3 6.7 %copy-start.6 = (bf16[512,4096]{1,0:T(8,128)(2,1)S(1)}, bf16[512,4096]{1,0:T(8,128)(2,1)}, u32[]{:S(2)}) copy-start(bf16[512,4096]{1,0:T(8,128)(2,1)} %param.19) | copy-start | bytes 12582916
  210.4 6.7 %copy-start.7 = (bf16[512,1376]{0,1:T(8,128)(2,1)S(1)}, bf16[512,1376]{0,1:T(8,128)(2,1)}, u32[]{:S(2)}) copy-start(bf16[512,1376]{0,1:T(8,128)(2,1)} %all-gather.7.cloned.1.call-done) | copy-start | bytes 4227076
  236.6 72.1 %copy-start.1 = (bf16[256,4096]{1,0:T(8,128)(2,1)S(1)}, bf16[256,4096]{1,0:T(8,128)(2,1)}, u32[]{:S(2)}) copy-start(bf16[256,4096]{1,0:T(8,128)(2,1)} %param.10) | copy-start | bytes 6291460
Sparse Core Ops, SparseCore 0:
  20.1 115.5 all-gather.4
  210.5 96.3 reduce-scatter.5
Sparse Core Ops, SparseCore 1:
  34.1 11.5 reduce-scatter.7
  172.4 11.8 reduce-scatter.3
  188.5 10.5 all-gather.6
  201.2 10.5 all-gather.8
  214.0 10.5 all-gather.10
where the time goes:
time: 317 us; the launch traced here: 316 us
  waiting for transfers between devices  177 us (56%)
  matrix products  74.5 us (24%)
  other arithmetic  24.8 us (8%)
  local copies, waits for them, and re-layouts  20.7 us (7%)
  between operations  15.9 us (5%)
    all_gather x1, waiting for transfers between devices, shards(): arrived = lax.all_gather(outgoing, 'dp', axis=0, tiled=True)  101 us
    reduce_scatter x1, waiting for transfers between devices, shards(): lax.psum_scatter(jnp.dot(block, w_down, preferred_element_type=jnp.float3...  59.3 us
    gather x1, local copies, waits for them, and re-layouts, shards(): train_rows = arrived[source_shard * shard_cap + shard_rank]  13 us
    dot_general x1, matrix products, shards(): lax.dot_general(block, w_down, (((1,), (1,)), ((), ())), preferred_elemen...  12.3 us
    dot_general x1, matrix products, shards(): jnp.dot(block, w_up, preferred_element_type=jnp.float32)  11.5 us
    dot_general x1, matrix products, shards(): jnp.dot(block, w_down, preferred_element_type=jnp.float32)  11.3 us
    dot_general x1, matrix products, shards(): lax.dot_general(block, lax.all_gather(up_delta, 'mp', axis=0, tiled=True)...  10.9 us
    dot_general x1, matrix products, shards(): lax.dot_general(block, lax.all_gather(gate_delta, 'mp', axis=0, tiled=Tru...  10.7 us
  transfers between devices with their start and end apart: 7, of which 4 were waited for; matrix products, arithmetic and copies ran while one was open for 32% of the time, Pallas kernels for 0%

commit v1 on v0

v1 whole, which is shorter than its diff:
```python
import jax
import jax.numpy as jnp
from jax import lax
from jax.sharding import PartitionSpec as P

D = 8192


epsilon = 1e-05


def rank_in_block(shard_blocks):
    size = shard_blocks.shape[1]
    same = shard_blocks[:, :, None] == shard_blocks[:, None, :]
    earlier = jnp.arange(size)[None, :, None] > jnp.arange(size)[None, None, :]
    return jnp.sum((same & earlier).astype(jnp.int32), axis=2)


def shards(
    store_rows, source_shard, source_row, state_len, visits, gain, w_gate, w_up, w_down, upstream
):
    count_dp = lax.axis_size("dp")
    count_mp = lax.axis_size("mp")
    index_dp = lax.axis_index("dp")
    index_mp = lax.axis_index("mp")
    total_rows = source_shard.shape[0]
    block_rows = total_rows // count_dp
    share_rows = total_rows // count_mp
    pair_cap = max(block_rows // 8, 1)
    width = store_rows.shape[1]
    half = width // 2
    layers = count_dp // 4
    share_first = index_mp * share_rows

    def across(value, mask):
        return lax.ppermute(value, "dp", [(i, i ^ mask) for i in range(count_dp)])

    def along(value, step):
        return lax.ppermute(
            value, "dp", [(i, (i + 4 * step) % count_dp) for i in range(count_dp)]
        )

    def scatter_sum(value):
        if count_mp != 2:
            return lax.psum_scatter(value, "mp", scatter_dimension=0, tiled=True).astype(
                jnp.float32
            )
        other = lax.dynamic_slice_in_dim(value, share_rows - share_first, share_rows, 0)
        other = lax.ppermute(other.astype(jnp.bfloat16), "mp", [(0, 1), (1, 0)])
        own = lax.dynamic_slice_in_dim(value, share_first, share_rows, 0)
        return own.astype(jnp.float32) + other.astype(jnp.float32)

    def join(value):
        if count_mp != 2:
            return lax.all_gather(value, "mp", axis=0, tiled=True)
        other = lax.ppermute(value, "mp", [(0, 1), (1, 0)])
        first = index_mp == 0
        return jnp.concatenate(
            [jnp.where(first, value, other), jnp.where(first, other, value)], axis=0
        )

    shard_blocks = source_shard.reshape(count_dp, block_rows)
    row_blocks = source_row.reshape(count_dp, block_rows)
    ranks = rank_in_block(shard_blocks)
    slots = jnp.arange(pair_cap, dtype=jnp.int32)
    given = (shard_blocks == index_dp)[:, None, :] & (ranks[:, None, :] == slots[None, :, None])
    chosen = jnp.sum(jnp.where(given, row_blocks[:, None, :] + 1, 0), axis=2).reshape(-1) - 1
    pick = (chosen[:, None] == jnp.arange(store_rows.shape[0])[None, :]).astype(jnp.bfloat16)
    outgoing = jnp.dot(pick, store_rows, preferred_element_type=jnp.float32).astype(jnp.bfloat16)
    arrived = lax.all_to_all(
        outgoing.reshape(count_dp, pair_cap, width), "dp", 0, 0, tiled=True
    ).reshape(count_dp * pair_cap, width)
    own_slot = (
        lax.dynamic_index_in_dim(shard_blocks, index_dp, 0, False) * pair_cap
        + lax.dynamic_index_in_dim(ranks, index_dp, 0, False)
    )
    place = (own_slot[:, None] == jnp.arange(count_dp * pair_cap)[None, :]).astype(jnp.bfloat16)
    own_rows = jnp.dot(place, arrived, preferred_element_type=jnp.float32).astype(jnp.bfloat16)
    own_float = own_rows.astype(jnp.float32)
    squares = jnp.sum(own_float * own_float, axis=1)
    squares_all = lax.all_gather(squares, ("dp", "mp"), axis=0, tiled=False)
    square_total = jnp.sum(squares_all.reshape(count_dp, count_mp, block_rows), axis=1)
    own_scaled = (own_float * gain.astype(jnp.float32)[None, :]).astype(jnp.bfloat16)

    near, over_y, over_x, over_xy = [], [], [], []
    for step in range(layers):
        block = own_scaled if step == 0 else along(own_scaled, step)
        block_y = across(block, 2)
        block_x = across(block, 1)
        block_xy = jnp.concatenate(
            [across(block_y[:, :half], 1), across(block_x[:, half:], 2)], axis=1
        )
        near.append(block)
        over_y.append(block_y)
        over_x.append(block_x)
        over_xy.append(block_xy)
    scaled = jnp.concatenate(near + over_y + over_x + over_xy, axis=0)
    order = []
    for mask in (0, 2, 1, 3):
        for step in range(layers):
            order.append(lax.rem(index_dp + 4 * (layers - step), count_dp) ^ mask)
    inverse = lax.rsqrt(square_total / D + epsilon)[jnp.stack(order)].reshape(total_rows)

    row_ids = jnp.arange(total_rows, dtype=jnp.int32)
    ends = jnp.cumsum(state_len)
    starts = ends - state_len
    member = ((row_ids[:, None] >= starts[None, :]) & (row_ids[:, None] < ends[None, :])).astype(
        jnp.float32
    )
    importance = jnp.log1p(visits.astype(jnp.float32))
    per_state = total_rows * importance / (state_len.astype(jnp.float32) * jnp.sum(importance))
    row_weight = jnp.sum(member * per_state[None, :], axis=1)
    weighted = (upstream.astype(jnp.float32) * row_weight[:, None]).astype(jnp.bfloat16)
    out_grad = jnp.concatenate(
        [lax.dynamic_slice_in_dim(weighted, b * block_rows, block_rows, 0) for b in order], axis=0
    )
    grad_hidden = scatter_sum(
        lax.dot_general(
            out_grad, w_down, (((1,), (1,)), ((), ())), preferred_element_type=jnp.float32
        ).astype(jnp.bfloat16)
    )

    inverse_share = lax.dynamic_slice_in_dim(inverse, share_first, share_rows, 0)
    gate_share = inverse_share[:, None] * scatter_sum(
        jnp.dot(scaled, w_gate, preferred_element_type=jnp.float32)
    )
    up_share = inverse_share[:, None] * scatter_sum(
        jnp.dot(scaled, w_up, preferred_element_type=jnp.float32)
    )
    sigmoid_gate = jax.nn.sigmoid(gate_share)
    hidden_all = join((gate_share * sigmoid_gate * up_share).astype(jnp.bfloat16))

    middle = total_rows // 2
    far_part = jnp.dot(
        hidden_all[middle:], w_down, preferred_element_type=jnp.float32
    ).astype(jnp.bfloat16)
    near_part = jnp.dot(
        hidden_all[:middle], w_down, preferred_element_type=jnp.float32
    ).astype(jnp.bfloat16)
    group = middle // 2
    from_x = across(far_part[group:, :half], 1).astype(jnp.float32)
    from_y = across(far_part[group:, half:], 2).astype(jnp.float32)
    part_x = far_part[:group].astype(jnp.float32)
    part_x = jnp.concatenate([part_x[:, :half], part_x[:, half:] + from_y], axis=1)
    part_y = near_part[group:].astype(jnp.float32)
    part_y = jnp.concatenate([part_y[:, :half] + from_x, part_y[:, half:]], axis=1)
    part_x = part_x.astype(jnp.bfloat16)
    part_y = part_y.astype(jnp.bfloat16)
    down_block = jnp.zeros((block_rows, width), jnp.float32)
    for step in list(range(1, layers)) + [0]:
        rows = slice(step * block_rows, (step + 1) * block_rows)
        summed = (
            near_part[rows].astype(jnp.float32)
            + across(part_x[rows], 1).astype(jnp.float32)
            + across(part_y[rows], 2).astype(jnp.float32)
        )
        if step > 0:
            summed = along(summed.astype(jnp.bfloat16), layers - step).astype(jnp.float32)
        down_block = down_block + summed
    layer_out = (own_float + down_block).astype(jnp.bfloat16)

    grad_down = lax.dot_general(
        hidden_all, out_grad, (((0,), (0,)), ((), ())), preferred_element_type=jnp.float32
    ).astype(jnp.bfloat16)
    gate_delta = (
        inverse_share[:, None]
        * grad_hidden
        * up_share
        * sigmoid_gate
        * (1.0 + gate_share * (1.0 - sigmoid_gate))
    ).astype(jnp.bfloat16)
    up_delta = (inverse_share[:, None] * grad_hidden * gate_share * sigmoid_gate).astype(
        jnp.bfloat16
    )
    grad_gate = lax.dot_general(
        scaled, join(gate_delta), (((0,), (0,)), ((), ())), preferred_element_type=jnp.float32
    ).astype(jnp.bfloat16)
    grad_up = lax.dot_general(
        scaled, join(up_delta), (((0,), (0,)), ((), ())), preferred_element_type=jnp.float32
    ).astype(jnp.bfloat16)
    return (layer_out, grad_gate, grad_up, grad_down)


def solution(mesh):
    in_specs = (
        P("dp", "mp"),
        P(),
        P(),
        P(),
        P(),
        P("mp"),
        P("mp", "dp"),
        P("mp", "dp"),
        P("dp", "mp"),
        P(None, "mp"),
    )
    out_specs = (P("dp", "mp"), P("mp", "dp"), P("mp", "dp"), P("dp", "mp"))
    return jax.shard_map(shards, mesh=mesh, in_specs=in_specs, out_specs=out_specs, check_vma=False)
```

time: 317 us -> 257 us (0.81)
  waiting for transfers between devices: 177 us -> 56.3 us
  starting transfers between devices: 0.7 us -> 44.2 us
  blocking collectives: 2.47 us -> 37.6 us
  between operations: 15.9 us -> 1.39 us
  local copies, waits for them, and re-layouts: 20.7 us -> 27.7 us
  other arithmetic: 24.8 us -> 18.7 us
  matrix products: 74.5 us -> 70.6 us
    all_gather x4 -> x0, waiting for transfers between devices: 110 us -> none  [the longest x1 101 us: shards(): arrived = lax.all_gather(outgoing, 'dp', axis=0, tiled=True)]
    reduce_scatter x3 -> x0, waiting for transfers between devices: 65.6 us -> none  [the longest x1 59.3 us: shards(): lax.psum_scatter(jnp.dot(block, w_down, preferred_element_type=jnp.float3...]
    ppermute x0 -> x38, waiting for transfers between devices: none -> 56.3 us  [the longest x26 33.2 us: across(): return lax.ppermute(value, 'dp', [(i, i ^ mask) for i in range(count_dp)])]
    unnamed x0 -> x1, blocking collectives: none -> 37.6 us
    ppermute x0 -> x38, starting transfers between devices: none -> 35.9 us  [the longest x26 25.3 us: across(): return lax.ppermute(value, 'dp', [(i, i ^ mask) for i in range(count_dp)])]
    unnamed x16 -> x62, local copies, waits for them, and re-layouts: 0.04 us -> 23.4 us
    gather x3 -> x1, local copies, waits for them, and re-layouts: 15.4 us -> 0.56 us  [shards(): lax.rsqrt(square_total / D + epsilon)[jnp.stack(order)].reshape(total_rows)]
    all_to_all x0 -> x1, starting transfers between devices: none -> 8.31 us  [shards(): lax.all_to_all(outgoing.reshape(count_dp, pair_cap, width), 'dp', 0, 0, t...]
  transfers between devices with their start and end apart: 7 -> 39, of which waited for: 4 -> 15; matrix products, arithmetic and copies ran while one was open for 32% -> 41% of each run, Pallas kernels for 0% -> 0%
where the time goes in v1:
time: 257 us
  matrix products  70.6 us (27%)
  waiting for transfers between devices  56.3 us (22%)
  starting transfers between devices  44.2 us (17%)
  blocking collectives  37.6 us (15%)
  local copies, waits for them, and re-layouts  27.7 us (11%)
  other arithmetic  18.7 us (7%)
    unnamed x1, blocking collectives  37.6 us
    ppermute x26, waiting for transfers between devices, across(): return lax.ppermute(value, 'dp', [(i, i ^ mask) for i in range(count_dp)])  33.2 us
    ppermute x26, starting transfers between devices, across(): return lax.ppermute(value, 'dp', [(i, i ^ mask) for i in range(count_dp)])  25.3 us
    unnamed x62, local copies, waits for them, and re-layouts  23.4 us
    ppermute x6, waiting for transfers between devices, along(): lax.ppermute(value, 'dp', [(i, (i + 4 * step) % count_dp) for i in range(...  20.2 us
    dot_general x1, matrix products, shards(): lax.dot_general(scaled, join(up_delta), (((0,), (0,)), ((), ())), preferr...  11.1 us
    dot_general x1, matrix products, shards(): lax.dot_general(hidden_all, out_grad, (((0,), (0,)), ((), ())), preferred...  10.9 us
    dot_general x1, matrix products, shards(): jnp.dot(scaled, w_up, preferred_element_type=jnp.float32)  10.4 us
  transfers between devices with their start and end apart: 39, of which 15 were waited for; matrix products, arithmetic and copies ran while one was open for 41% of the time, Pallas kernels for 0%

profile of v1, /device:TPU:0, one launch (start us, length us, event | category | flops | bytes accessed | tf_op | source)
XLA Modules:
  0.0 256.5 jit_solution(10358685165203994907)
XLA Ops:
  4.7 8.3 %all-to-all-start = ((bf16[16,4,4096]{2,1,0:T(4,128)(2,1)}), bf16[16,4,4096]{2,1,0:T(4,128)(2,1)S(1)}, u32[]{:S(2)}, u32[]{:S(2)}) async-start(bf16[16,4,4096]{2,1,0:T(4,128)(2,1)} %reshape.722), calls=%async_computation | async-start | bytes 1048576 | tf_op jit(solution)/shard_map/all_to_all | solution.py:70
  14.8 3.7 %multiply_convert_fusion = bf16[512,4096]{1,0:T(8,128)(2,1)S(1)} fusion(bf16[512,4096]{1,0:T(8,128)(2,1)} %param.19, f32[512]{0:T(512)S(1)} %select_reduce_fusion), kind=kLoop, calls=%fused_computation.4 | loop fusion | flops 6291456 | bytes 8390656 | tf_op jit(solution)/shard_map/convert_element_type | solution.py:113
  31.3 1.8 collective-permute-start.7
  34.6 3.3 %collective-permute-start.2 = (bf16[32,4096]{1,0:T(8,128)(2,1)}, bf16[32,4096]{1,0:T(8,128)(2,1)}, u32[]{:S(2)}, u32[]{:S(2)}) collective-permute-start(bf16[32,4096]{1,0:T(8,128)(2,1)} %get-tuple-element.5), channel_id=1, source_target_pairs={{0,24},{2,26},{4,28},{6,30},{8,0},{10,2},{12,4},{14,6},{16,8},{18,... | collective-permute-start | bytes 786440 | tf_op jit(solution)/shard_map/ppermute | solution.py:39
  37.9 10.1 %convolution_convert_fusion.7 = bf16[512,1376]{0,1:T(8,128)(2,1)S(1)} fusion(bf16[512,4096]{1,0:T(8,128)(2,1)} %dynamic-slice_dynamic-update-slice_fusion, bf16[1376,4096]{1,0:T(8,128)(2,1)} %param.18), kind=kOutput, calls=%fused_computation.10 | convolution fusion | flops 5772066816 | bytes 16875520 | tf_op jit(solution)/shard_map/dot_general | solution.py:118
  52.1 1.7 constant_dynamic-update-slice_fusion.10
  53.8 9.8 %collective-permute-done.1 = bf16[32,4096]{1,0:T(8,128)(2,1)S(1)} collective-permute-done((bf16[32,4096]{1,0:T(8,128)(2,1)}, bf16[32,4096]{1,0:T(8,128)(2,1)S(1)}, u32[]{:S(2)}, u32[]{:S(2)}) %collective-permute-start.1) | collective-permute-done | bytes 262176 | tf_op jit(solution)/shard_map/ppermute | solution.py:39
  64.9 1.7 constant_dynamic-update-slice_fusion.8
  66.5 1.7 constant_dynamic-update-slice_fusion.7
  72.9 5.7 %collective-permute-done.5 = bf16[32,4096]{1,0:T(8,128)(2,1)S(1)} collective-permute-done((bf16[32,4096]{1,0:T(8,128)(2,1)S(1)}, bf16[32,4096]{1,0:T(8,128)(2,1)S(1)}, u32[]{:S(2)}, u32[]{:S(2)}) %collective-permute-start.5) | collective-permute-done | bytes 262176 | tf_op jit(solution)/shard_map/ppermute | solution.py:36
  81.3 3.9 %collective-permute-done.8 = bf16[32,4096]{1,0:T(8,128)(2,1)S(1)} collective-permute-done((bf16[32,4096]{1,0:T(8,128)(2,1)}, bf16[32,4096]{1,0:T(8,128)(2,1)S(1)}, u32[]{:S(2)}, u32[]{:S(2)}) %collective-permute-start.8) | collective-permute-done | bytes 262176 | tf_op jit(solution)/shard_map/ppermute | solution.py:36
  92.3 2.6 %collective-permute-done.14 = bf16[32,2048]{1,0:T(8,128)(2,1)S(1)} collective-permute-done((bf16[32,2048]{1,0:T(8,128)(2,1)S(1)}, bf16[32,2048]{1,0:T(8,128)(2,1)S(1)}, u32[]{:S(2)}, u32[]{:S(2)}) %collective-permute-start.14) | collective-permute-done | bytes 131104 | tf_op jit(solution)/shard_map/ppermute | solution.py:36
  102.8 10.4 %fusion.30 = f32[512,1376]{0,1:T(8,128)S(1)} fusion(bf16[512,4096]{1,0:T(8,128)(2,1)} %maximum_dynamic-update-slice_fusion, bf16[4096,1376]{0,1:T(8,128)(2,1)} %param.17), kind=kOutput, calls=%fused_computation.129 | convolution fusion | flops 5771362304 | bytes 18284544 | tf_op jit(solution)/shard_map/dot_general | solution.py:128
  113.5 6.0 %fusion.29 = f32[512,1376]{0,1:T(8,128)S(1)} fusion(bf16[512,4096]{1,0:T(8,128)(2,1)S(1)} %copy-done.6, bf16[4096,1376]{0,1:T(8,128)(2,1)S(1)} %bitcast.40), kind=kOutput, calls=%fused_computation.128 | convolution fusion | flops 5771362304 | bytes 18284544 | tf_op jit(solution)/shard_map/dot_general | solution.py:125
  122.1 37.6 %all-reduce = f32[1024]{0:T(1024)S(1)} all-reduce(f32[1024]{0:T(1024)S(1)} %dynamic-update-slice), channel_id=2, replica_groups=mesh['dp'=16,'mp'=2] {'dp','mp'}, use_global_device_ids=true, to_apply=%add | all-reduce | flops 1024 | bytes 8192
  160.6 4.7 %multiply_convert_fusion.2 = (bf16[256,1376]{0,1:T(8,128)(2,1)S(1)}, bf16[256,1376]{0,1:T(8,128)(2,1)S(1)}, bf16[256,1376]{0,1:T(8,128)(2,1)}) fusion(bf16[256,1376]{0,1:T(8,128)(2,1)} %collective-permute-done.35, bf16[256,1376]{0,1:T(8,128)(2,1)} %collective-permute-done.20, f32[512,1376]{0,1:T(8,128)} %copy-done.2, s32[]{:T(128)S(6)} %select_n.110, ...), kind=kLoop, calls=%fused_computation.21 | loop fusion | flops 9158656 | bytes 7750660 | tf_op jit(solution)/shard_map/convert_element_type | solution.py:171
  165.7 2.8 %collective-permute-done.21 = bf16[256,1376]{0,1:T(8,128)(2,1)} collective-permute-done((bf16[256,1376]{0,1:T(8,128)(2,1)S(1)}, bf16[256,1376]{0,1:T(8,128)(2,1)}, u32[]{:S(2)}, u32[]{:S(2)}) %collective-permute-start.21) | collective-permute-done | bytes 704544 | tf_op jit(solution)/shard_map/ppermute | solution.py:56
  169.7 7.9 %convolution_convert_fusion.3 = bf16[256,4096]{1,0:T(8,128)(2,1)S(1)} fusion(bf16[256,1376]{0,1:T(8,128)(2,1)S(1)} %get-tuple-element.19, bf16[1376,4096]{1,0:T(8,128)(2,1)} %param.18), kind=kOutput, calls=%fused_computation.5 | convolution fusion | flops 2886729728 | bytes 14073856 | tf_op jit(solution)/shard_map/dot_general | solution.py:134
  177.8 2.3 collective-permute-start.24
  180.1 2.0 collective-permute-start.22
  182.1 10.9 %convolution_convert_fusion.2 = bf16[1376,4096]{1,0:T(8,128)(2,1)} fusion(bf16[512,4096]{1,0:T(8,128)(2,1)} %dynamic-slice_dynamic-update-slice_fusion, bf16[256,1376]{0,1:T(8,128)(2,1)S(1)} %get-tuple-element.19, bf16[256,1376]{0,1:T(8,128)(2,1)S(1)} %get-tuple-element.20), kind=kOutput, calls=%fused_computation.3 | convolution fusion | flops 5779816448 | bytes 16875520 | tf_op jit(solution)/shard_map/dot_general | solution.py:162
  194.4 11.1 %convolution_convert_fusion = bf16[4096,1376]{0,1:T(8,128)(2,1)} fusion(bf16[512,4096]{1,0:T(8,128)(2,1)} %maximum_dynamic-update-slice_fusion, bf16[256,1376]{0,1:T(8,128)(2,1)S(1)} %get-tuple-element.16, bf16[256,1376]{0,1:T(8,128)(2,1)S(1)} %get-tuple-element.15), kind=kOutput, calls=%fused_computation.1 | convolution fusion | flops 5779816448 | bytes 16875520 | tf_op jit(solution)/shard_map/dot_general | solution.py:178
  205.5 3.9 %convolution_convert_fusion.4 = bf16[256,4096]{1,0:T(8,128)(2,1)S(1)} fusion(bf16[256,1376]{0,1:T(8,128)(2,1)S(1)} %get-tuple-element.20, bf16[1376,4096]{1,0:T(8,128)(2,1)S(1)} %bitcast.37), kind=kOutput, calls=%fused_computation.6 | convolution fusion | flops 2886729728 | bytes 14073856 | tf_op jit(solution)/shard_map/dot_general | solution.py:137
  209.8 2.0 collective-permute-start.28
  212.2 1.9 collective-permute-start.27
  214.2 4.8 %collective-permute-done.25 = bf16[32,4096]{1,0:T(8,128)(2,1)S(1)} collective-permute-done((bf16[32,4096]{1,0:T(8,128)(2,1)S(1)}, bf16[32,4096]{1,0:T(8,128)(2,1)S(1)}, u32[]{:S(2)}, u32[]{:S(2)}) %collective-permute-start.25) | collective-permute-done | bytes 262176 | tf_op jit(solution)/shard_map/ppermute | solution.py:36
  219.1 5.5 %collective-permute-done.28 = bf16[32,4096]{1,0:T(8,128)(2,1)S(1)} collective-permute-done((bf16[32,4096]{1,0:T(8,128)(2,1)S(1)}, bf16[32,4096]{1,0:T(8,128)(2,1)S(1)}, u32[]{:S(2)}, u32[]{:S(2)}) %collective-permute-start.28) | collective-permute-done | bytes 262176 | tf_op jit(solution)/shard_map/ppermute | solution.py:36
  224.6 5.6 %collective-permute-done.31 = bf16[32,4096]{1,0:T(8,128)(2,1)S(1)} collective-permute-done((bf16[32,4096]{1,0:T(8,128)(2,1)S(1)}, bf16[32,4096]{1,0:T(8,128)(2,1)S(1)}, u32[]{:S(2)}, u32[]{:S(2)}) %collective-permute-start.31) | collective-permute-done | bytes 262176 | tf_op jit(solution)/shard_map/ppermute | solution.py:36
  233.7 2.8 %collective-permute-start.29 = (bf16[32,4096]{1,0:T(8,128)(2,1)S(1)}, bf16[32,4096]{1,0:T(8,128)(2,1)S(1)}, u32[]{:S(2)}, u32[]{:S(2)}) collective-permute-start(bf16[32,4096]{1,0:T(8,128)(2,1)S(1)} %get-tuple-element.11), channel_id=1, source_target_pairs={{0,16},{2,18},{4,20},{6,22},{8,24},{10,26},{12,28},{14,30},{16,0},... | collective-permute-start | bytes 786440 | tf_op jit(solution)/shard_map/ppermute | solution.py:39
  236.4 8.7 %convolution_convert_fusion.1 = bf16[4096,1376]{0,1:T(8,128)(2,1)} fusion(bf16[512,4096]{1,0:T(8,128)(2,1)S(1)} %copy-done.7, bf16[256,1376]{0,1:T(8,128)(2,1)S(1)} %get-tuple-element.18, bf16[256,1376]{0,1:T(8,128)(2,1)S(1)} %get-tuple-element.17), kind=kOutput, calls=%fused_computation.2 | convolution fusion | flops 5779816448 | bytes 16875520 | tf_op jit(solution)/shard_map/dot_general | solution.py:175
  245.2 2.9 %collective-permute-done.32 = bf16[32,4096]{1,0:T(8,128)(2,1)S(1)} collective-permute-done((bf16[32,4096]{1,0:T(8,128)(2,1)S(1)}, bf16[32,4096]{1,0:T(8,128)(2,1)S(1)}, u32[]{:S(2)}, u32[]{:S(2)}) %collective-permute-start.32) | collective-permute-done | bytes 262176 | tf_op jit(solution)/shard_map/ppermute | solution.py:39
  248.0 7.6 %collective-permute-done.29 = bf16[32,4096]{1,0:T(8,128)(2,1)S(1)} collective-permute-done((bf16[32,4096]{1,0:T(8,128)(2,1)S(1)}, bf16[32,4096]{1,0:T(8,128)(2,1)S(1)}, u32[]{:S(2)}, u32[]{:S(2)}) %collective-permute-start.29) | collective-permute-done | bytes 262176 | tf_op jit(solution)/shard_map/ppermute | solution.py:39
  (181 shorter events, 59.6 us)
Async XLA Ops:
  4.7 25.4 %all-to-all-start = ((bf16[16,4,4096]{2,1,0:T(4,128)(2,1)}), bf16[16,4,4096]{2,1,0:T(4,128)(2,1)S(1)}, u32[]{:S(2)}, u32[]{:S(2)}) async-start(bf16[16,4,4096]{2,1,0:T(4,128)(2,1)} %reshape.722), calls=%async_computation | async-start | bytes 1048576 | tf_op jit(solution)/shard_map/all_to_all | solution.py:70
  31.3 16.8 %collective-permute-start.7 = (bf16[32,4096]{1,0:T(8,128)(2,1)}, bf16[32,4096]{1,0:T(8,128)(2,1)S(1)}, u32[]{:S(2)}, u32[]{:S(2)}) collective-permute-start(bf16[32,4096]{1,0:T(8,128)(2,1)} %get-tuple-element.5), channel_id=1, source_target_pairs={{0,2},{2,0},{4,6},{6,4},{8,10},{10,8},{12,14},{14,12},{16,18},{18,... | collective-permute-start | bytes 786440 | tf_op jit(solution)/shard_map/ppermute | solution.py:36
  33.1 16.2 %collective-permute-start.3 = (bf16[32,4096]{1,0:T(8,128)(2,1)}, bf16[32,4096]{1,0:T(8,128)(2,1)S(1)}, u32[]{:S(2)}, u32[]{:S(2)}) collective-permute-start(bf16[32,4096]{1,0:T(8,128)(2,1)} %get-tuple-element.5), channel_id=1, source_target_pairs={{0,4},{2,6},{4,0},{6,2},{8,12},{10,14},{12,8},{14,10},{16,20},{18,... | collective-permute-start | bytes 786440 | tf_op jit(solution)/shard_map/ppermute | solution.py:36
  34.6 15.5 %collective-permute-start.2 = (bf16[32,4096]{1,0:T(8,128)(2,1)}, bf16[32,4096]{1,0:T(8,128)(2,1)}, u32[]{:S(2)}, u32[]{:S(2)}) collective-permute-start(bf16[32,4096]{1,0:T(8,128)(2,1)} %get-tuple-element.5), channel_id=1, source_target_pairs={{0,24},{2,26},{4,28},{6,30},{8,0},{10,2},{12,4},{14,6},{16,8},{18,... | collective-permute-start | bytes 786440 | tf_op jit(solution)/shard_map/ppermute | solution.py:39
  37.9 12.8 %collective-permute-start = (bf16[32,4096]{1,0:T(8,128)(2,1)}, bf16[32,4096]{1,0:T(8,128)(2,1)}, u32[]{:S(2)}, u32[]{:S(2)}) collective-permute-start(bf16[32,4096]{1,0:T(8,128)(2,1)} %get-tuple-element.5), channel_id=1, source_target_pairs={{0,8},{2,10},{4,12},{6,14},{8,16},{10,18},{12,20},{14,22},{16,24},... | collective-permute-start | bytes 786440 | tf_op jit(solution)/shard_map/ppermute | solution.py:39
  48.1 112.5 %collective-permute-start.35 = (bf16[256,1376]{0,1:T(8,128)(2,1)S(1)}, bf16[256,1376]{0,1:T(8,128)(2,1)}, u32[]{:S(2)}, u32[]{:S(2)}) collective-permute-start(bf16[256,1376]{0,1:T(8,128)(2,1)S(1)} %constant_dynamic-slice_fusion), channel_id=1, source_target_pairs={{0,1},{1,0},{2,3},{3,2},{4,5},{5,4},{6,7},{7,6},{8,9},{9,8},{10,11... | collective-permute-start | bytes 2113544 | tf_op jit(solution)/shard_map/ppermute | solution.py:49
  48.1 15.4 %collective-permute-start.1 = (bf16[32,4096]{1,0:T(8,128)(2,1)}, bf16[32,4096]{1,0:T(8,128)(2,1)S(1)}, u32[]{:S(2)}, u32[]{:S(2)}) collective-permute-start(bf16[32,4096]{1,0:T(8,128)(2,1)} %get-tuple-element.5), channel_id=1, source_target_pairs={{0,16},{2,18},{4,20},{6,22},{8,24},{10,26},{12,28},{14,30},{16,0},... | collective-permute-start | bytes 786440 | tf_op jit(solution)/shard_map/ppermute | solution.py:39
  49.4 39.2 %collective-permute-start.12 = (bf16[32,2048]{1,0:T(8,128)(2,1)S(1)}, bf16[32,2048]{1,0:T(8,128)(2,1)S(1)}, u32[]{:S(2)}, u32[]{:S(2)}) collective-permute-start(bf16[32,2048]{1,0:T(8,128)(2,1)S(1)} %slice.123), channel_id=1, source_target_pairs={{0,4},{2,6},{4,0},{6,2},{8,12},{10,14},{12,8},{14,10},{16,20},{18,... | collective-permute-start | bytes 393224 | tf_op jit(solution)/shard_map/ppermute | solution.py:36
  50.1 18.1 %collective-permute-start.10 = (bf16[32,4096]{1,0:T(8,128)(2,1)}, bf16[32,4096]{1,0:T(8,128)(2,1)S(1)}, u32[]{:S(2)}, u32[]{:S(2)}) collective-permute-start(bf16[32,4096]{1,0:T(8,128)(2,1)} %collective-permute-done.2), channel_id=1, source_target_pairs={{0,2},{2,0},{4,6},{6,4},{8,10},{10,8},{12,14},{14,12},{16,18},{18,... | collective-permute-start | bytes 786440 | tf_op jit(solution)/shard_map/ppermute | solution.py:36
  50.7 18.1 %collective-permute-start.6 = (bf16[32,4096]{1,0:T(8,128)(2,1)}, bf16[32,4096]{1,0:T(8,128)(2,1)S(1)}, u32[]{:S(2)}, u32[]{:S(2)}) collective-permute-start(bf16[32,4096]{1,0:T(8,128)(2,1)} %collective-permute-done.2), channel_id=1, source_target_pairs={{0,4},{2,6},{4,0},{6,2},{8,12},{10,14},{12,8},{14,10},{16,20},{18,... | collective-permute-start | bytes 786440 | tf_op jit(solution)/shard_map/ppermute | solution.py:36
  63.6 8.1 %collective-permute-start.4 = (bf16[32,4096]{1,0:T(8,128)(2,1)}, bf16[32,4096]{1,0:T(8,128)(2,1)S(1)}, u32[]{:S(2)}, u32[]{:S(2)}) collective-permute-start(bf16[32,4096]{1,0:T(8,128)(2,1)} %collective-permute-done), channel_id=1, source_target_pairs={{0,4},{2,6},{4,0},{6,2},{8,12},{10,14},{12,8},{14,10},{16,20},{18,... | collective-permute-start | bytes 786440 | tf_op jit(solution)/shard_map/ppermute | solution.py:36
  68.2 21.9 %collective-permute-start.11 = (bf16[32,2048]{1,0:T(8,128)(2,1)S(1)}, bf16[32,2048]{1,0:T(8,128)(2,1)S(1)}, u32[]{:S(2)}, u32[]{:S(2)}) collective-permute-start(bf16[32,2048]{1,0:T(8,128)(2,1)S(1)} %slice.122), channel_id=1, source_target_pairs={{0,2},{2,0},{4,6},{6,4},{8,10},{10,8},{12,14},{14,12},{16,18},{18,... | collective-permute-start | bytes 393224 | tf_op jit(solution)/shard_map/ppermute | solution.py:36
  68.8 17.7 %collective-permute-start.9 = (bf16[32,4096]{1,0:T(8,128)(2,1)S(1)}, bf16[32,4096]{1,0:T(8,128)(2,1)S(1)}, u32[]{:S(2)}, u32[]{:S(2)}) collective-permute-start(bf16[32,4096]{1,0:T(8,128)(2,1)S(1)} %collective-permute-done.1), channel_id=1, source_target_pairs={{0,2},{2,0},{4,6},{6,4},{8,10},{10,8},{12,14},{14,12},{16,18},{18,... | collective-permute-start | bytes 786440 | tf_op jit(solution)/shard_map/ppermute | solution.py:36
  85.2 16.9 %collective-permute-start.18 = (bf16[32,2048]{1,0:T(8,128)(2,1)S(1)}, bf16[32,2048]{1,0:T(8,128)(2,1)S(1)}, u32[]{:S(2)}, u32[]{:S(2)}) collective-permute-start(bf16[32,2048]{1,0:T(8,128)(2,1)S(1)} %slice.129), channel_id=1, source_target_pairs={{0,4},{2,6},{4,0},{6,2},{8,12},{10,14},{12,8},{14,10},{16,20},{18,... | collective-permute-start | bytes 393224 | tf_op jit(solution)/shard_map/ppermute | solution.py:36
  86.5 15.6 %collective-permute-start.17 = (bf16[32,2048]{1,0:T(8,128)(2,1)S(1)}, bf16[32,2048]{1,0:T(8,128)(2,1)S(1)}, u32[]{:S(2)}, u32[]{:S(2)}) collective-permute-start(bf16[32,2048]{1,0:T(8,128)(2,1)S(1)} %slice.128), channel_id=1, source_target_pairs={{0,2},{2,0},{4,6},{6,4},{8,10},{10,8},{12,14},{14,12},{16,18},{18,... | collective-permute-start | bytes 393224 | tf_op jit(solution)/shard_map/ppermute | solution.py:36
  113.4 47.2 %collective-permute-start.20 = (bf16[256,1376]{0,1:T(8,128)(2,1)S(1)}, bf16[256,1376]{0,1:T(8,128)(2,1)}, u32[]{:S(2)}, u32[]{:S(2)}) collective-permute-start(bf16[256,1376]{0,1:T(8,128)(2,1)S(1)} %dynamic-slice_convert_fusion), channel_id=1, source_target_pairs={{0,1},{1,0},{2,3},{3,2},{4,5},{5,4},{6,7},{7,6},{8,9},{9,8},{10,11... | collective-permute-start | bytes 2113544 | tf_op jit(solution)/shard_map/ppermute | solution.py:49
  121.1 39.5 %collective-permute-start.19 = (bf16[256,1376]{0,1:T(8,128)(2,1)S(1)}, bf16[256,1376]{0,1:T(8,128)(2,1)}, u32[]{:S(2)}, u32[]{:S(2)}) collective-permute-start(bf16[256,1376]{0,1:T(8,128)(2,1)S(1)} %dynamic-slice_convert_fusion.1), channel_id=1, source_target_pairs={{0,1},{1,0},{2,3},{3,2},{4,5},{5,4},{6,7},{7,6},{8,9},{9,8},{10,11... | collective-permute-start | bytes 2113544 | tf_op jit(solution)/shard_map/ppermute | solution.py:49
  165.2 47.0 %collective-permute-start.36 = (bf16[256,1376]{0,1:T(8,128)(2,1)S(1)}, bf16[256,1376]{0,1:T(8,128)(2,1)S(1)}, u32[]{:S(2)}, u32[]{:S(2)}) collective-permute-start(bf16[256,1376]{0,1:T(8,128)(2,1)S(1)} %get-tuple-element.6), channel_id=1, source_target_pairs={{0,1},{1,0},{2,3},{3,2},{4,5},{5,4},{6,7},{7,6},{8,9},{9,8},{10,11... | collective-permute-start | bytes 2113544 | tf_op jit(solution)/shard_map/ppermute | solution.py:56
  165.7 27.3 %collective-permute-start.37 = (bf16[256,1376]{0,1:T(8,128)(2,1)}, bf16[256,1376]{0,1:T(8,128)(2,1)S(1)}, u32[]{:S(2)}, u32[]{:S(2)}) collective-permute-start(bf16[256,1376]{0,1:T(8,128)(2,1)} %get-tuple-element.8), channel_id=1, source_target_pairs={{0,1},{1,0},{2,3},{3,2},{4,5},{5,4},{6,7},{7,6},{8,9},{9,8},{10,11... | collective-permute-start | bytes 2113544 | tf_op jit(solution)/shard_map/ppermute | solution.py:56
  177.8 31.6 %collective-permute-start.24 = (bf16[128,2048]{1,0:T(8,128)(2,1)S(1)}, bf16[128,2048]{1,0:T(8,128)(2,1)S(1)}, u32[]{:S(2)}, u32[]{:S(2)}) collective-permute-start(bf16[128,2048]{1,0:T(8,128)(2,1)S(1)} %get-tuple-element.13), channel_id=1, source_target_pairs={{0,2},{2,0},{4,6},{6,4},{8,10},{10,8},{12,14},{14,12},{16,18},{18,... | collective-permute-start | bytes 1572872 | tf_op jit(solution)/shard_map/ppermute | solution.py:36
  180.1 31.7 %collective-permute-start.22 = (bf16[128,2048]{1,0:T(8,128)(2,1)S(1)}, bf16[128,2048]{1,0:T(8,128)(2,1)S(1)}, u32[]{:S(2)}, u32[]{:S(2)}) collective-permute-start(bf16[128,2048]{1,0:T(8,128)(2,1)S(1)} %get-tuple-element.14), channel_id=1, source_target_pairs={{0,4},{2,6},{4,0},{6,2},{8,12},{10,14},{12,8},{14,10},{16,20},{18,... | collective-permute-start | bytes 1572872 | tf_op jit(solution)/shard_map/ppermute | solution.py:36
  209.7 9.3 %collective-permute-start.25 = (bf16[32,4096]{1,0:T(8,128)(2,1)S(1)}, bf16[32,4096]{1,0:T(8,128)(2,1)S(1)}, u32[]{:S(2)}, u32[]{:S(2)}) collective-permute-start(bf16[32,4096]{1,0:T(8,128)(2,1)S(1)} %get-tuple-element.25), channel_id=1, source_target_pairs={{0,4},{2,6},{4,0},{6,2},{8,12},{10,14},{12,8},{14,10},{16,20},{18,... | collective-permute-start | bytes 786440 | tf_op jit(solution)/shard_map/ppermute | solution.py:36
  209.8 14.8 %collective-permute-start.28 = (bf16[32,4096]{1,0:T(8,128)(2,1)S(1)}, bf16[32,4096]{1,0:T(8,128)(2,1)S(1)}, u32[]{:S(2)}, u32[]{:S(2)}) collective-permute-start(bf16[32,4096]{1,0:T(8,128)(2,1)S(1)} %get-tuple-element.26), channel_id=1, source_target_pairs={{0,4},{2,6},{4,0},{6,2},{8,12},{10,14},{12,8},{14,10},{16,20},{18,... | collective-permute-start | bytes 786440 | tf_op jit(solution)/shard_map/ppermute | solution.py:36
  211.8 18.4 %collective-permute-start.31 = (bf16[32,4096]{1,0:T(8,128)(2,1)S(1)}, bf16[32,4096]{1,0:T(8,128)(2,1)S(1)}, u32[]{:S(2)}, u32[]{:S(2)}) collective-permute-start(bf16[32,4096]{1,0:T(8,128)(2,1)S(1)} %get-tuple-element.28), channel_id=1, source_target_pairs={{0,4},{2,6},{4,0},{6,2},{8,12},{10,14},{12,8},{14,10},{16,20},{18,... | collective-permute-start | bytes 786440 | tf_op jit(solution)/shard_map/ppermute | solution.py:36
  212.1 18.2 %collective-permute-start.23 = (bf16[32,4096]{1,0:T(8,128)(2,1)S(1)}, bf16[32,4096]{1,0:T(8,128)(2,1)S(1)}, u32[]{:S(2)}, u32[]{:S(2)}) collective-permute-start(bf16[32,4096]{1,0:T(8,128)(2,1)S(1)} %get-tuple-element.21), channel_id=1, source_target_pairs={{0,2},{2,0},{4,6},{6,4},{8,10},{10,8},{12,14},{14,12},{16,18},{18,... | collective-permute-start | bytes 786440 | tf_op jit(solution)/shard_map/ppermute | solution.py:36
  212.2 18.0 %collective-permute-start.27 = (bf16[32,4096]{1,0:T(8,128)(2,1)S(1)}, bf16[32,4096]{1,0:T(8,128)(2,1)S(1)}, u32[]{:S(2)}, u32[]{:S(2)}) collective-permute-start(bf16[32,4096]{1,0:T(8,128)(2,1)S(1)} %get-tuple-element.22), channel_id=1, source_target_pairs={{0,2},{2,0},{4,6},{6,4},{8,10},{10,8},{12,14},{14,12},{16,18},{18,... | collective-permute-start | bytes 786440 | tf_op jit(solution)/shard_map/ppermute | solution.py:36
  219.0 12.2 %collective-permute-start.30 = (bf16[32,4096]{1,0:T(8,128)(2,1)S(1)}, bf16[32,4096]{1,0:T(8,128)(2,1)S(1)}, u32[]{:S(2)}, u32[]{:S(2)}) collective-permute-start(bf16[32,4096]{1,0:T(8,128)(2,1)S(1)} %get-tuple-element.24), channel_id=1, source_target_pairs={{0,2},{2,0},{4,6},{6,4},{8,10},{10,8},{12,14},{14,12},{16,18},{18,... | collective-permute-start | bytes 786440 | tf_op jit(solution)/shard_map/ppermute | solution.py:36
  224.6 20.6 %collective-permute-start.34 = (bf16[32,4096]{1,0:T(8,128)(2,1)S(1)}, bf16[32,4096]{1,0:T(8,128)(2,1)S(1)}, u32[]{:S(2)}, u32[]{:S(2)}) collective-permute-start(bf16[32,4096]{1,0:T(8,128)(2,1)S(1)} %get-tuple-element.27), channel_id=1, source_target_pairs={{0,4},{2,6},{4,0},{6,2},{8,12},{10,14},{12,8},{14,10},{16,20},{18,... | collective-permute-start | bytes 786440 | tf_op jit(solution)/shard_map/ppermute | solution.py:36
  230.2 15.0 %collective-permute-start.33 = (bf16[32,4096]{1,0:T(8,128)(2,1)S(1)}, bf16[32,4096]{1,0:T(8,128)(2,1)S(1)}, u32[]{:S(2)}, u32[]{:S(2)}) collective-permute-start(bf16[32,4096]{1,0:T(8,128)(2,1)S(1)} %get-tuple-element.23), channel_id=1, source_target_pairs={{0,2},{2,0},{4,6},{6,4},{8,10},{10,8},{12,14},{14,12},{16,18},{18,... | collective-permute-start | bytes 786440 | tf_op jit(solution)/shard_map/ppermute | solution.py:36
  231.4 13.8 %collective-permute-start.26 = (bf16[32,4096]{1,0:T(8,128)(2,1)S(1)}, bf16[32,4096]{1,0:T(8,128)(2,1)S(1)}, u32[]{:S(2)}, u32[]{:S(2)}) collective-permute-start(bf16[32,4096]{1,0:T(8,128)(2,1)S(1)} %get-tuple-element.9), channel_id=1, source_target_pairs={{0,24},{2,26},{4,28},{6,30},{8,0},{10,2},{12,4},{14,6},{16,8},{18,... | collective-permute-start | bytes 786440 | tf_op jit(solution)/shard_map/ppermute | solution.py:39
  233.0 15.0 %collective-permute-start.32 = (bf16[32,4096]{1,0:T(8,128)(2,1)S(1)}, bf16[32,4096]{1,0:T(8,128)(2,1)S(1)}, u32[]{:S(2)}, u32[]{:S(2)}) collective-permute-start(bf16[32,4096]{1,0:T(8,128)(2,1)S(1)} %get-tuple-element.10), channel_id=1, source_target_pairs={{0,8},{2,10},{4,12},{6,14},{8,16},{10,18},{12,20},{14,22},{16,24},... | collective-permute-start | bytes 786440 | tf_op jit(solution)/shard_map/ppermute | solution.py:39
  233.7 21.9 %collective-permute-start.29 = (bf16[32,4096]{1,0:T(8,128)(2,1)S(1)}, bf16[32,4096]{1,0:T(8,128)(2,1)S(1)}, u32[]{:S(2)}, u32[]{:S(2)}) collective-permute-start(bf16[32,4096]{1,0:T(8,128)(2,1)S(1)} %get-tuple-element.11), channel_id=1, source_target_pairs={{0,16},{2,18},{4,20},{6,22},{8,24},{10,26},{12,28},{14,30},{16,0},... | collective-permute-start | bytes 786440 | tf_op jit(solution)/shard_map/ppermute | solution.py:39
  (24 other events, 257.3 us)

commit v2 on v1

--- a/solution.py
+++ b/solution.py
@@ -28,7 +28,6 @@
     share_rows = total_rows // count_mp
     pair_cap = max(block_rows // 8, 1)
     width = store_rows.shape[1]
-    half = width // 2
     layers = count_dp // 4
     share_first = index_mp * share_rows
 
@@ -78,8 +77,15 @@
     own_rows = jnp.dot(place, arrived, preferred_element_type=jnp.float32).astype(jnp.bfloat16)
     own_float = own_rows.astype(jnp.float32)
     squares = jnp.sum(own_float * own_float, axis=1)
-    squares_all = lax.all_gather(squares, ("dp", "mp"), axis=0, tiled=False)
-    square_total = jnp.sum(squares_all.reshape(count_dp, count_mp, block_rows), axis=1)
+    squares = jnp.concatenate(
+        [squares] + [along(squares, step) for step in range(1, layers)], axis=0
+    )
+    squares = jnp.concatenate([squares, across(squares, 2)], axis=0)
+    squares = jnp.concatenate([squares, across(squares, 1)], axis=0)
+    if count_mp == 2:
+        square_total = squares + lax.ppermute(squares, "mp", [(0, 1), (1, 0)])
+    else:
+        square_total = lax.psum(squares, "mp")
     own_scaled = (own_float * gain.astype(jnp.float32)[None, :]).astype(jnp.bfloat16)
 
     near, over_y, over_x, over_xy = [], [], [], []
@@ -87,19 +93,18 @@
         block = own_scaled if step == 0 else along(own_scaled, step)
         block_y = across(block, 2)
         block_x = across(block, 1)
-        block_xy = jnp.concatenate(
-            [across(block_y[:, :half], 1), across(block_x[:, half:], 2)], axis=1
-        )
+        block_xy = across(block_y, 1) if step % 2 == 0 else across(block_x, 2)
         near.append(block)
         over_y.append(block_y)
         over_x.append(block_x)
         over_xy.append(block_xy)
     scaled = jnp.concatenate(near + over_y + over_x + over_xy, axis=0)
+    scaled, square_total = lax.optimization_barrier((scaled, square_total))
     order = []
     for mask in (0, 2, 1, 3):
         for step in range(layers):
             order.append(lax.rem(index_dp + 4 * (layers - step), count_dp) ^ mask)
-    inverse = lax.rsqrt(square_total / D + epsilon)[jnp.stack(order)].reshape(total_rows)
+    inverse = lax.rsqrt(square_total / D + epsilon)
 
     row_ids = jnp.arange(total_rows, dtype=jnp.int32)
     ends = jnp.cumsum(state_len)
@@ -138,21 +143,32 @@
         hidden_all[:middle], w_down, preferred_element_type=jnp.float32
     ).astype(jnp.bfloat16)
     group = middle // 2
-    from_x = across(far_part[group:, :half], 1).astype(jnp.float32)
-    from_y = across(far_part[group:, half:], 2).astype(jnp.float32)
-    part_x = far_part[:group].astype(jnp.float32)
-    part_x = jnp.concatenate([part_x[:, :half], part_x[:, half:] + from_y], axis=1)
-    part_y = near_part[group:].astype(jnp.float32)
-    part_y = jnp.concatenate([part_y[:, :half] + from_x, part_y[:, half:]], axis=1)
-    part_x = part_x.astype(jnp.bfloat16)
-    part_y = part_y.astype(jnp.bfloat16)
+    summed_x, summed_y = [], []
+    parts_xy = [
+        far_part[group + step * block_rows : group + (step + 1) * block_rows]
+        for step in range(layers)
+    ]
+    parts_xy, near_part, hidden_late = lax.optimization_barrier((parts_xy, near_part, hidden_all))
+    steps = list(range(1, layers)) + [0]
+    for step in steps:
+        rows = slice(step * block_rows, (step + 1) * block_rows)
+        part_x = far_part[:group][rows]
+        part_y = near_part[group:][rows]
+        part_xy = parts_xy[step]
+        if step % 2 == 0:
+            part_y = part_y.astype(jnp.float32) + across(part_xy, 1).astype(jnp.float32)
+        else:
+            part_x = part_x.astype(jnp.float32) + across(part_xy, 2).astype(jnp.float32)
+        summed_x.append(part_x.astype(jnp.bfloat16))
+        summed_y.append(part_y.astype(jnp.bfloat16))
+    summed_x, summed_y, scaled_late = lax.optimization_barrier((summed_x, summed_y, scaled))
     down_block = jnp.zeros((block_rows, width), jnp.float32)
-    for step in list(range(1, layers)) + [0]:
+    for step, part_x, part_y in zip(steps, summed_x, summed_y):
         rows = slice(step * block_rows, (step + 1) * block_rows)
         summed = (
             near_part[rows].astype(jnp.float32)
-            + across(part_x[rows], 1).astype(jnp.float32)
-            + across(part_y[rows], 2).astype(jnp.float32)
+            + across(part_x, 1).astype(jnp.float32)
+            + across(part_y, 2).astype(jnp.float32)
         )
         if step > 0:
             summed = along(summed.astype(jnp.bfloat16), layers - step).astype(jnp.float32)
@@ -160,7 +176,7 @@
     layer_out = (own_float + down_block).astype(jnp.bfloat16)
 
     grad_down = lax.dot_general(
-        hidden_all, out_grad, (((0,), (0,)), ((), ())), preferred_element_type=jnp.float32
+        hidden_late, out_grad, (((0,), (0,)), ((), ())), preferred_element_type=jnp.float32
     ).astype(jnp.bfloat16)
     gate_delta = (
         inverse_share[:, None]
@@ -173,10 +189,10 @@
         jnp.bfloat16
     )
     grad_gate = lax.dot_general(
-        scaled, join(gate_delta), (((0,), (0,)), ((), ())), preferred_element_type=jnp.float32
+        scaled_late, join(gate_delta), (((0,), (0,)), ((), ())), preferred_element_type=jnp.float32
     ).astype(jnp.bfloat16)
     grad_up = lax.dot_general(
-        scaled, join(up_delta), (((0,), (0,)), ((), ())), preferred_element_type=jnp.float32
+        scaled_late, join(up_delta), (((0,), (0,)), ((), ())), preferred_element_type=jnp.float32
     ).astype(jnp.bfloat16)
     return (layer_out, grad_gate, grad_up, grad_down)
 

time: 257 us -> 225 us (0.88)
  blocking collectives: 37.6 us -> 0 us
  starting transfers between devices: 44.2 us -> 51.2 us
  other arithmetic: 18.7 us -> 14.9 us
  waiting for transfers between devices: 56.3 us -> 59.8 us
    unnamed x1 -> x0, blocking collectives: 37.6 us -> none
    ppermute x26, starting transfers between devices: 25.3 us -> 28.8 us  [across(): return lax.ppermute(value, 'dp', [(i, i ^ mask) for i in range(count_dp)])]
    ppermute x6 -> x9, starting transfers between devices: 9.47 us -> 12.2 us  [along(): lax.ppermute(value, 'dp', [(i, (i + 4 * step) % count_dp) for i in range(...]
    ppermute x6 -> x9, waiting for transfers between devices: 20.2 us -> 22.4 us  [along(): lax.ppermute(value, 'dp', [(i, (i + 4 * step) % count_dp) for i in range(...]
    unnamed x62 -> x63, local copies, waits for them, and re-layouts: 23.4 us -> 22.9 us
  transfers between devices with their start and end apart: 39 -> 43, of which waited for: 15 -> 18; matrix products, arithmetic and copies ran while one was open for 41% -> 45% of each run, Pallas kernels for 0% -> 0%
where the time goes in v2:
time: 225 us
  matrix products  69.7 us (31%)
  waiting for transfers between devices  59.8 us (27%)
  starting transfers between devices  51.2 us (23%)
  local copies, waits for them, and re-layouts  28.2 us (13%)
  other arithmetic  14.9 us (7%)
    ppermute x26, waiting for transfers between devices, across(): return lax.ppermute(value, 'dp', [(i, i ^ mask) for i in range(count_dp)])  34.2 us
    ppermute x26, starting transfers between devices, across(): return lax.ppermute(value, 'dp', [(i, i ^ mask) for i in range(count_dp)])  28.8 us
    unnamed x63, local copies, waits for them, and re-layouts  22.9 us
    ppermute x9, waiting for transfers between devices, along(): lax.ppermute(value, 'dp', [(i, (i + 4 * step) % count_dp) for i in range(...  22.4 us
    ppermute x9, starting transfers between devices, along(): lax.ppermute(value, 'dp', [(i, (i + 4 * step) % count_dp) for i in range(...  12.2 us
    dot_general x1, matrix products, shards(): jnp.dot(scaled, w_up, preferred_element_type=jnp.float32)  11.7 us
    dot_general x1, matrix products, shards(): lax.dot_general(hidden_late, out_grad, (((0,), (0,)), ((), ())), preferre...  10.9 us
    dot_general x1, matrix products, shards(): lax.dot_general(out_grad, w_down, (((1,), (1,)), ((), ())), preferred_ele...  10.1 us
  transfers between devices with their start and end apart: 43, of which 18 were waited for; matrix products, arithmetic and copies ran while one was open for 45% of the time, Pallas kernels for 0%

profile of v2, /device:TPU:0, one launch (start us, length us, event | category | flops | bytes accessed | tf_op | source)
XLA Modules:
  0.0 225.1 jit_solution(4226507014797655353)
XLA Ops:
  4.7 8.3 %all-to-all-start = ((bf16[16,4,4096]{2,1,0:T(4,128)(2,1)}), bf16[16,4,4096]{2,1,0:T(4,128)(2,1)S(1)}, u32[]{:S(2)}, u32[]{:S(2)}) async-start(bf16[16,4,4096]{2,1,0:T(4,128)(2,1)} %reshape.99), calls=%async_computation | async-start | bytes 1048576 | tf_op jit(solution)/shard_map/all_to_all | solution.py:69
  14.8 3.7 %multiply_convert_fusion = bf16[512,4096]{1,0:T(8,128)(2,1)S(1)} fusion(bf16[512,4096]{1,0:T(8,128)(2,1)} %param.19, f32[512]{0:T(512)S(1)} %select_reduce_fusion), kind=kLoop, calls=%fused_computation.3 | loop fusion | flops 6291456 | bytes 8390656 | tf_op jit(solution)/shard_map/convert_element_type | solution.py:118
  31.3 3.7 %collective-permute-start.17 = (f32[32]{0:T(128)S(1)}, f32[32]{0:T(128)S(1)}, u32[]{:S(2)}, u32[]{:S(2)}) collective-permute-start(f32[32]{0:T(128)S(1)} %multiply_reduce_fusion), channel_id=1, source_target_pairs={{0,24},{2,26},{4,28},{6,30},{8,0},{10,2},{12,4},{14,6},{16,8},{18,... | collective-permute-start | bytes 392 | tf_op jit(solution)/shard_map/ppermute | solution.py:38
  36.3 3.1 %collective-permute-done.16 = f32[32]{0:T(128)S(1)} collective-permute-done((f32[32]{0:T(128)S(1)}, f32[32]{0:T(128)S(1)}, u32[]{:S(2)}, u32[]{:S(2)}) %collective-permute-start.16) | collective-permute-done | bytes 160 | tf_op jit(solution)/shard_map/ppermute | solution.py:38
  41.8 1.7 dynamic-slice_dynamic-update-slice_fusion
  45.5 10.1 %convolution_convert_fusion.7 = bf16[512,1376]{0,1:T(8,128)(2,1)S(1)} fusion(bf16[512,4096]{1,0:T(8,128)(2,1)} %dynamic-slice_dynamic-update-slice_fusion, bf16[1376,4096]{1,0:T(8,128)(2,1)} %param.18), kind=kOutput, calls=%fused_computation.9 | convolution fusion | flops 5772066816 | bytes 16875520 | tf_op jit(solution)/shard_map/dot_general | solution.py:123
  58.3 2.5 %collective-permute-start.2 = (bf16[32,4096]{1,0:T(8,128)(2,1)}, bf16[32,4096]{1,0:T(8,128)(2,1)S(1)}, u32[]{:S(2)}, u32[]{:S(2)}) collective-permute-start(bf16[32,4096]{1,0:T(8,128)(2,1)} %get-tuple-element.39), channel_id=1, source_target_pairs={{0,24},{2,26},{4,28},{6,30},{8,0},{10,2},{12,4},{14,6},{16,8},{18,... | collective-permute-start | bytes 786440 | tf_op jit(solution)/shard_map/ppermute | solution.py:38
  61.6 3.5 %collective-permute-done.3 = bf16[32,4096]{1,0:T(8,128)(2,1)S(1)} collective-permute-done((bf16[32,4096]{1,0:T(8,128)(2,1)}, bf16[32,4096]{1,0:T(8,128)(2,1)S(1)}, u32[]{:S(2)}, u32[]{:S(2)}) %collective-permute-start.3) | collective-permute-done | bytes 262176 | tf_op jit(solution)/shard_map/ppermute | solution.py:35
  67.9 1.5 collective-permute-start.11
  69.4 8.0 %collective-permute-done.1 = bf16[32,4096]{1,0:T(8,128)(2,1)S(1)} collective-permute-done((bf16[32,4096]{1,0:T(8,128)(2,1)}, bf16[32,4096]{1,0:T(8,128)(2,1)S(1)}, u32[]{:S(2)}, u32[]{:S(2)}) %collective-permute-start.1) | collective-permute-done | bytes 262176 | tf_op jit(solution)/shard_map/ppermute | solution.py:38
  81.0 1.5 collective-permute-start.5
  83.1 4.3 %collective-permute-done.5 = bf16[32,4096]{1,0:T(8,128)(2,1)S(1)} collective-permute-done((bf16[32,4096]{1,0:T(8,128)(2,1)S(1)}, bf16[32,4096]{1,0:T(8,128)(2,1)S(1)}, u32[]{:S(2)}, u32[]{:S(2)}) %collective-permute-start.5) | collective-permute-done | bytes 262176 | tf_op jit(solution)/shard_map/ppermute | solution.py:35
  87.5 1.5 collective-permute-start.6
  89.7 4.2 %collective-permute-done.6 = bf16[32,4096]{1,0:T(8,128)(2,1)S(1)} collective-permute-done((bf16[32,4096]{1,0:T(8,128)(2,1)S(1)}, bf16[32,4096]{1,0:T(8,128)(2,1)S(1)}, u32[]{:S(2)}, u32[]{:S(2)}) %collective-permute-start.6) | collective-permute-done | bytes 262176 | tf_op jit(solution)/shard_map/ppermute | solution.py:35
  97.3 8.6 %collective-permute-done.8 = bf16[32,4096]{1,0:T(8,128)(2,1)S(1)} collective-permute-done((bf16[32,4096]{1,0:T(8,128)(2,1)S(1)}, bf16[32,4096]{1,0:T(8,128)(2,1)S(1)}, u32[]{:S(2)}, u32[]{:S(2)}) %collective-permute-start.8) | collective-permute-done | bytes 262176 | tf_op jit(solution)/shard_map/ppermute | solution.py:35
  111.6 2.2 collective-permute-done.12
  117.3 11.7 %fusion.20 = f32[512,1376]{0,1:T(8,128)S(1)} fusion(bf16[512,4096]{1,0:T(8,128)(2,1)} %constant_dynamic-update-slice_fusion, bf16[4096,1376]{0,1:T(8,128)(2,1)} %param.17), kind=kOutput, calls=%fused_computation.106 | convolution fusion | flops 5771362304 | bytes 18284544 | tf_op jit(solution)/shard_map/dot_general | solution.py:133
  129.3 6.0 %fusion.19 = f32[512,1376]{0,1:T(8,128)S(1)} fusion(bf16[512,4096]{1,0:T(8,128)(2,1)S(1)} %copy-done.6, bf16[4096,1376]{0,1:T(8,128)(2,1)S(1)} %bitcast.23), kind=kOutput, calls=%fused_computation.105 | convolution fusion | flops 5771362304 | bytes 18284544 | tf_op jit(solution)/shard_map/dot_general | solution.py:130
  137.4 1.8 collective-permute-done.21
  139.3 4.6 %multiply_convert_fusion.2 = (bf16[256,1376]{0,1:T(8,128)(2,1)}, bf16[256,1376]{0,1:T(8,128)(2,1)S(1)}, bf16[256,1376]{0,1:T(8,128)(2,1)S(1)}) fusion(bf16[256,1376]{0,1:T(8,128)(2,1)} %collective-permute-done.39, bf16[256,1376]{0,1:T(8,128)(2,1)} %collective-permute-done.22, f32[512,1376]{0,1:T(8,128)} %copy-done.3, s32[]{:T(128)S(6)} %select_n.99, ...), kind=kLoop, calls=%fused_computation.18 | loop fusion | flops 9158656 | bytes 7750660 | tf_op jit(solution)/shard_map/convert_element_type | solution.py:187
  146.2 8.1 %convolution_convert_fusion.4 = bf16[256,4096]{1,0:T(8,128)(2,1)S(1)} fusion(bf16[256,1376]{0,1:T(8,128)(2,1)S(1)} %get-tuple-element.63, bf16[1376,4096]{1,0:T(8,128)(2,1)} %param.18), kind=kOutput, calls=%fused_computation.5 | convolution fusion | flops 2886729728 | bytes 14073856 | tf_op jit(solution)/shard_map/dot_general | solution.py:139
  154.4 3.9 %convolution_convert_fusion.3 = bf16[256,4096]{1,0:T(8,128)(2,1)S(1)} fusion(bf16[256,1376]{0,1:T(8,128)(2,1)S(1)} %get-tuple-element.62, bf16[1376,4096]{1,0:T(8,128)(2,1)S(1)} %bitcast.20), kind=kOutput, calls=%fused_computation.4 | convolution fusion | flops 2886729728 | bytes 14073856 | tf_op jit(solution)/shard_map/dot_general | solution.py:142
  161.9 10.9 %convolution_convert_fusion.2 = bf16[1376,4096]{1,0:T(8,128)(2,1)} fusion(bf16[512,1376]{0,1:T(8,128)(2,1)S(1)} %pad_maximum_fusion, bf16[512,4096]{1,0:T(8,128)(2,1)} %dynamic-slice_dynamic-update-slice_fusion), kind=kOutput, calls=%fused_computation.2 | convolution fusion | flops 5776998400 | bytes 16875520 | tf_op jit(solution)/shard_map/dot_general | solution.py:178
  173.6 1.6 broadcast_select_fusion.3
  175.3 5.3 %collective-permute-done.27 = bf16[32,4096]{1,0:T(8,128)(2,1)S(1)} collective-permute-done((bf16[32,4096]{1,0:T(8,128)(2,1)S(1)}, bf16[32,4096]{1,0:T(8,128)(2,1)S(1)}, u32[]{:S(2)}, u32[]{:S(2)}) %collective-permute-start.27) | collective-permute-done | bytes 262176 | tf_op jit(solution)/shard_map/ppermute | solution.py:35
  183.0 1.5 collective-permute-start.31
  185.7 4.3 %collective-permute-done.28 = bf16[32,4096]{1,0:T(8,128)(2,1)S(1)} collective-permute-done((bf16[32,4096]{1,0:T(8,128)(2,1)S(1)}, bf16[32,4096]{1,0:T(8,128)(2,1)S(1)}, u32[]{:S(2)}, u32[]{:S(2)}) %collective-permute-start.28) | collective-permute-done | bytes 262176 | tf_op jit(solution)/shard_map/ppermute | solution.py:35
  190.0 1.5 collective-permute-start.35
  191.5 8.7 %convolution_convert_fusion.1 = bf16[4096,1376]{0,1:T(8,128)(2,1)} fusion(bf16[512,4096]{1,0:T(8,128)(2,1)S(1)} %copy-done.7, bf16[256,1376]{0,1:T(8,128)(2,1)S(1)} %get-tuple-element.61, bf16[256,1376]{0,1:T(8,128)(2,1)S(1)} %get-tuple-element.60), kind=kOutput, calls=%fused_computation.1 | convolution fusion | flops 5779816448 | bytes 16875520 | tf_op jit(solution)/shard_map/dot_general | solution.py:191
  201.8 4.2 %collective-permute-start.30 = (bf16[32,4096]{1,0:T(8,128)(2,1)S(1)}, bf16[32,4096]{1,0:T(8,128)(2,1)S(1)}, u32[]{:S(2)}, u32[]{:S(2)}) collective-permute-start(bf16[32,4096]{1,0:T(8,128)(2,1)S(1)} %get-tuple-element.43), channel_id=1, source_target_pairs={{0,24},{2,26},{4,28},{6,30},{8,0},{10,2},{12,4},{14,6},{16,8},{18,... | collective-permute-start | bytes 786440 | tf_op jit(solution)/shard_map/ppermute | solution.py:38
  206.6 8.7 %convolution_convert_fusion = bf16[4096,1376]{0,1:T(8,128)(2,1)} fusion(bf16[512,4096]{1,0:T(8,128)(2,1)S(1)} %copy-done.7, bf16[256,1376]{0,1:T(8,128)(2,1)S(1)} %get-tuple-element.59, bf16[256,1376]{0,1:T(8,128)(2,1)S(1)} %get-tuple-element.58), kind=kOutput, calls=%fused_computation | convolution fusion | flops 5779816448 | bytes 16875520 | tf_op jit(solution)/shard_map/dot_general | solution.py:194
  216.6 7.5 %collective-permute-done.33 = bf16[32,4096]{1,0:T(8,128)(2,1)S(1)} collective-permute-done((bf16[32,4096]{1,0:T(8,128)(2,1)S(1)}, bf16[32,4096]{1,0:T(8,128)(2,1)S(1)}, u32[]{:S(2)}, u32[]{:S(2)}) %collective-permute-start.33) | collective-permute-done | bytes 262176 | tf_op jit(solution)/shard_map/ppermute | solution.py:38
  (174 shorter events, 65.1 us)
Async XLA Ops:
  4.7 25.2 %all-to-all-start = ((bf16[16,4,4096]{2,1,0:T(4,128)(2,1)}), bf16[16,4,4096]{2,1,0:T(4,128)(2,1)S(1)}, u32[]{:S(2)}, u32[]{:S(2)}) async-start(bf16[16,4,4096]{2,1,0:T(4,128)(2,1)} %reshape.99), calls=%async_computation | async-start | bytes 1048576 | tf_op jit(solution)/shard_map/all_to_all | solution.py:69
  43.5 17.3 %collective-permute-start = (bf16[32,4096]{1,0:T(8,128)(2,1)}, bf16[32,4096]{1,0:T(8,128)(2,1)S(1)}, u32[]{:S(2)}, u32[]{:S(2)}) collective-permute-start(bf16[32,4096]{1,0:T(8,128)(2,1)} %get-tuple-element.39), channel_id=1, source_target_pairs={{0,8},{2,10},{4,12},{6,14},{8,16},{10,18},{12,20},{14,22},{16,24},... | collective-permute-start | bytes 786440 | tf_op jit(solution)/shard_map/ppermute | solution.py:38
  44.0 11.6 %collective-permute-start.19 = (f32[256]{0:T(256)S(1)}, f32[256]{0:T(256)S(1)}, u32[]{:S(2)}, u32[]{:S(2)}) collective-permute-start(f32[256]{0:T(256)S(1)} %concatenate.28), channel_id=1, source_target_pairs={{0,2},{2,0},{4,6},{6,4},{8,10},{10,8},{12,14},{14,12},{16,18},{18,... | collective-permute-start | bytes 3080 | tf_op jit(solution)/shard_map/ppermute | solution.py:35
  55.8 81.7 %collective-permute-start.39 = (bf16[256,1376]{0,1:T(8,128)(2,1)S(1)}, bf16[256,1376]{0,1:T(8,128)(2,1)}, u32[]{:S(2)}, u32[]{:S(2)}) collective-permute-start(bf16[256,1376]{0,1:T(8,128)(2,1)S(1)} %constant_dynamic-slice_fusion), channel_id=1, source_target_pairs={{0,1},{1,0},{2,3},{3,2},{4,5},{5,4},{6,7},{7,6},{8,9},{9,8},{10,11... | collective-permute-start | bytes 2113544 | tf_op jit(solution)/shard_map/ppermute | solution.py:48
  56.3 39.0 %collective-permute-start.7 = (bf16[32,4096]{1,0:T(8,128)(2,1)}, bf16[32,4096]{1,0:T(8,128)(2,1)S(1)}, u32[]{:S(2)}, u32[]{:S(2)}) collective-permute-start(bf16[32,4096]{1,0:T(8,128)(2,1)} %get-tuple-element.39), channel_id=1, source_target_pairs={{0,2},{2,0},{4,6},{6,4},{8,10},{10,8},{12,14},{14,12},{16,18},{18,... | collective-permute-start | bytes 786440 | tf_op jit(solution)/shard_map/ppermute | solution.py:35
  56.9 8.2 %collective-permute-start.3 = (bf16[32,4096]{1,0:T(8,128)(2,1)}, bf16[32,4096]{1,0:T(8,128)(2,1)S(1)}, u32[]{:S(2)}, u32[]{:S(2)}) collective-permute-start(bf16[32,4096]{1,0:T(8,128)(2,1)} %get-tuple-element.39), channel_id=1, source_target_pairs={{0,4},{2,6},{4,0},{6,2},{8,12},{10,14},{12,8},{14,10},{16,20},{18,... | collective-permute-start | bytes 786440 | tf_op jit(solution)/shard_map/ppermute | solution.py:35
  58.3 9.6 %collective-permute-start.2 = (bf16[32,4096]{1,0:T(8,128)(2,1)}, bf16[32,4096]{1,0:T(8,128)(2,1)S(1)}, u32[]{:S(2)}, u32[]{:S(2)}) collective-permute-start(bf16[32,4096]{1,0:T(8,128)(2,1)} %get-tuple-element.39), channel_id=1, source_target_pairs={{0,24},{2,26},{4,28},{6,30},{8,0},{10,2},{12,4},{14,6},{16,8},{18,... | collective-permute-start | bytes 786440 | tf_op jit(solution)/shard_map/ppermute | solution.py:38
  60.9 16.5 %collective-permute-start.1 = (bf16[32,4096]{1,0:T(8,128)(2,1)}, bf16[32,4096]{1,0:T(8,128)(2,1)S(1)}, u32[]{:S(2)}, u32[]{:S(2)}) collective-permute-start(bf16[32,4096]{1,0:T(8,128)(2,1)} %get-tuple-element.39), channel_id=1, source_target_pairs={{0,16},{2,18},{4,20},{6,22},{8,24},{10,26},{12,28},{14,30},{16,0},... | collective-permute-start | bytes 786440 | tf_op jit(solution)/shard_map/ppermute | solution.py:38
  65.1 15.9 %collective-permute-start.4 = (bf16[32,4096]{1,0:T(8,128)(2,1)S(1)}, bf16[32,4096]{1,0:T(8,128)(2,1)S(1)}, u32[]{:S(2)}, u32[]{:S(2)}) collective-permute-start(bf16[32,4096]{1,0:T(8,128)(2,1)S(1)} %collective-permute-done), channel_id=1, source_target_pairs={{0,4},{2,6},{4,0},{6,2},{8,12},{10,14},{12,8},{14,10},{16,20},{18,... | collective-permute-start | bytes 786440 | tf_op jit(solution)/shard_map/ppermute | solution.py:35
  67.9 42.9 %collective-permute-start.11 = (bf16[32,4096]{1,0:T(8,128)(2,1)S(1)}, bf16[32,4096]{1,0:T(8,128)(2,1)S(1)}, u32[]{:S(2)}, u32[]{:S(2)}) collective-permute-start(bf16[32,4096]{1,0:T(8,128)(2,1)S(1)} %collective-permute-done.3), channel_id=1, source_target_pairs={{0,2},{2,0},{4,6},{6,4},{8,10},{10,8},{12,14},{14,12},{16,18},{18,... | collective-permute-start | bytes 786440 | tf_op jit(solution)/shard_map/ppermute | solution.py:35
  77.4 30.0 %collective-permute-start.10 = (bf16[32,4096]{1,0:T(8,128)(2,1)S(1)}, bf16[32,4096]{1,0:T(8,128)(2,1)S(1)}, u32[]{:S(2)}, u32[]{:S(2)}) collective-permute-start(bf16[32,4096]{1,0:T(8,128)(2,1)S(1)} %collective-permute-done.2), channel_id=1, source_target_pairs={{0,2},{2,0},{4,6},{6,4},{8,10},{10,8},{12,14},{14,12},{16,18},{18,... | collective-permute-start | bytes 786440 | tf_op jit(solution)/shard_map/ppermute | solution.py:35
  93.9 14.9 %collective-permute-start.9 = (bf16[32,4096]{1,0:T(8,128)(2,1)S(1)}, bf16[32,4096]{1,0:T(8,128)(2,1)S(1)}, u32[]{:S(2)}, u32[]{:S(2)}) collective-permute-start(bf16[32,4096]{1,0:T(8,128)(2,1)S(1)} %collective-permute-done.1), channel_id=1, source_target_pairs={{0,2},{2,0},{4,6},{6,4},{8,10},{10,8},{12,14},{14,12},{16,18},{18,... | collective-permute-start | bytes 786440 | tf_op jit(solution)/shard_map/ppermute | solution.py:35
  95.3 10.7 %collective-permute-start.8 = (bf16[32,4096]{1,0:T(8,128)(2,1)S(1)}, bf16[32,4096]{1,0:T(8,128)(2,1)S(1)}, u32[]{:S(2)}, u32[]{:S(2)}) collective-permute-start(bf16[32,4096]{1,0:T(8,128)(2,1)S(1)} %collective-permute-done), channel_id=1, source_target_pairs={{0,2},{2,0},{4,6},{6,4},{8,10},{10,8},{12,14},{14,12},{16,18},{18,... | collective-permute-start | bytes 786440 | tf_op jit(solution)/shard_map/ppermute | solution.py:35
  106.0 8.5 %collective-permute-start.13 = (bf16[32,4096]{1,0:T(8,128)(2,1)S(1)}, bf16[32,4096]{1,0:T(8,128)(2,1)S(1)}, u32[]{:S(2)}, u32[]{:S(2)}) collective-permute-start(bf16[32,4096]{1,0:T(8,128)(2,1)S(1)} %collective-permute-done.5), channel_id=1, source_target_pairs={{0,2},{2,0},{4,6},{6,4},{8,10},{10,8},{12,14},{14,12},{16,18},{18,... | collective-permute-start | bytes 786440 | tf_op jit(solution)/shard_map/ppermute | solution.py:35
  108.7 7.8 %collective-permute-start.14 = (bf16[32,4096]{1,0:T(8,128)(2,1)S(1)}, bf16[32,4096]{1,0:T(8,128)(2,1)S(1)}, u32[]{:S(2)}, u32[]{:S(2)}) collective-permute-start(bf16[32,4096]{1,0:T(8,128)(2,1)S(1)} %collective-permute-done.10), channel_id=1, source_target_pairs={{0,4},{2,6},{4,0},{6,2},{8,12},{10,14},{12,8},{14,10},{16,20},{18,... | collective-permute-start | bytes 786440 | tf_op jit(solution)/shard_map/ppermute | solution.py:35
  129.2 8.3 %collective-permute-start.22 = (bf16[256,1376]{0,1:T(8,128)(2,1)S(1)}, bf16[256,1376]{0,1:T(8,128)(2,1)}, u32[]{:S(2)}, u32[]{:S(2)}) collective-permute-start(bf16[256,1376]{0,1:T(8,128)(2,1)S(1)} %dynamic-slice_convert_fusion), channel_id=1, source_target_pairs={{0,1},{1,0},{2,3},{3,2},{4,5},{5,4},{6,7},{7,6},{8,9},{9,8},{10,11... | collective-permute-start | bytes 2113544 | tf_op jit(solution)/shard_map/ppermute | solution.py:48
  144.3 28.5 %collective-permute-start.40 = (bf16[256,1376]{0,1:T(8,128)(2,1)}, bf16[256,1376]{0,1:T(8,128)(2,1)S(1)}, u32[]{:S(2)}, u32[]{:S(2)}) collective-permute-start(bf16[256,1376]{0,1:T(8,128)(2,1)} %get-tuple-element.40), channel_id=1, source_target_pairs={{0,1},{1,0},{2,3},{3,2},{4,5},{5,4},{6,7},{7,6},{8,9},{9,8},{10,11... | collective-permute-start | bytes 2113544 | tf_op jit(solution)/shard_map/ppermute | solution.py:55
  144.4 37.1 %collective-permute-start.41 = (bf16[256,1376]{0,1:T(8,128)(2,1)S(1)}, bf16[256,1376]{0,1:T(8,128)(2,1)S(1)}, u32[]{:S(2)}, u32[]{:S(2)}) collective-permute-start(bf16[256,1376]{0,1:T(8,128)(2,1)S(1)} %get-tuple-element.42), channel_id=1, source_target_pairs={{0,1},{1,0},{2,3},{3,2},{4,5},{5,4},{6,7},{7,6},{8,9},{9,8},{10,11... | collective-permute-start | bytes 2113544 | tf_op jit(solution)/shard_map/ppermute | solution.py:55
  158.5 16.7 %collective-permute-start.24 = (bf16[32,4096]{1,0:T(8,128)(2,1)S(1)}, bf16[32,4096]{1,0:T(8,128)(2,1)S(1)}, u32[]{:S(2)}, u32[]{:S(2)}) collective-permute-start(bf16[32,4096]{1,0:T(8,128)(2,1)S(1)} %get-tuple-element.24), channel_id=1, source_target_pairs={{0,4},{2,6},{4,0},{6,2},{8,12},{10,14},{12,8},{14,10},{16,20},{18,... | collective-permute-start | bytes 786440 | tf_op jit(solution)/shard_map/ppermute | solution.py:35
  159.8 15.3 %collective-permute-start.25 = (bf16[32,4096]{1,0:T(8,128)(2,1)S(1)}, bf16[32,4096]{1,0:T(8,128)(2,1)S(1)}, u32[]{:S(2)}, u32[]{:S(2)}) collective-permute-start(bf16[32,4096]{1,0:T(8,128)(2,1)S(1)} %get-tuple-element.25), channel_id=1, source_target_pairs={{0,4},{2,6},{4,0},{6,2},{8,12},{10,14},{12,8},{14,10},{16,20},{18,... | collective-permute-start | bytes 786440 | tf_op jit(solution)/shard_map/ppermute | solution.py:35
  160.5 14.8 %collective-permute-start.26 = (bf16[32,4096]{1,0:T(8,128)(2,1)S(1)}, bf16[32,4096]{1,0:T(8,128)(2,1)S(1)}, u32[]{:S(2)}, u32[]{:S(2)}) collective-permute-start(bf16[32,4096]{1,0:T(8,128)(2,1)S(1)} %get-tuple-element.26), channel_id=1, source_target_pairs={{0,2},{2,0},{4,6},{6,4},{8,10},{10,8},{12,14},{14,12},{16,18},{18,... | collective-permute-start | bytes 786440 | tf_op jit(solution)/shard_map/ppermute | solution.py:35
  180.7 9.3 %collective-permute-start.28 = (bf16[32,4096]{1,0:T(8,128)(2,1)S(1)}, bf16[32,4096]{1,0:T(8,128)(2,1)S(1)}, u32[]{:S(2)}, u32[]{:S(2)}) collective-permute-start(bf16[32,4096]{1,0:T(8,128)(2,1)S(1)} %get-tuple-element.28), channel_id=1, source_target_pairs={{0,2},{2,0},{4,6},{6,4},{8,10},{10,8},{12,14},{14,12},{16,18},{18,... | collective-permute-start | bytes 786440 | tf_op jit(solution)/shard_map/ppermute | solution.py:35
  181.6 18.6 %collective-permute-start.29 = (bf16[32,4096]{1,0:T(8,128)(2,1)S(1)}, bf16[32,4096]{1,0:T(8,128)(2,1)S(1)}, u32[]{:S(2)}, u32[]{:S(2)}) collective-permute-start(bf16[32,4096]{1,0:T(8,128)(2,1)S(1)} %get-tuple-element.29), channel_id=1, source_target_pairs={{0,4},{2,6},{4,0},{6,2},{8,12},{10,14},{12,8},{14,10},{16,20},{18,... | collective-permute-start | bytes 786440 | tf_op jit(solution)/shard_map/ppermute | solution.py:35
  183.0 17.8 %collective-permute-start.31 = (bf16[32,4096]{1,0:T(8,128)(2,1)S(1)}, bf16[32,4096]{1,0:T(8,128)(2,1)S(1)}, u32[]{:S(2)}, u32[]{:S(2)}) collective-permute-start(bf16[32,4096]{1,0:T(8,128)(2,1)S(1)} %get-tuple-element.30), channel_id=1, source_target_pairs={{0,2},{2,0},{4,6},{6,4},{8,10},{10,8},{12,14},{14,12},{16,18},{18,... | collective-permute-start | bytes 786440 | tf_op jit(solution)/shard_map/ppermute | solution.py:35
  184.4 17.0 %collective-permute-start.32 = (bf16[32,4096]{1,0:T(8,128)(2,1)S(1)}, bf16[32,4096]{1,0:T(8,128)(2,1)S(1)}, u32[]{:S(2)}, u32[]{:S(2)}) collective-permute-start(bf16[32,4096]{1,0:T(8,128)(2,1)S(1)} %get-tuple-element.31), channel_id=1, source_target_pairs={{0,4},{2,6},{4,0},{6,2},{8,12},{10,14},{12,8},{14,10},{16,20},{18,... | collective-permute-start | bytes 786440 | tf_op jit(solution)/shard_map/ppermute | solution.py:35
  185.0 16.5 %collective-permute-start.34 = (bf16[32,4096]{1,0:T(8,128)(2,1)S(1)}, bf16[32,4096]{1,0:T(8,128)(2,1)S(1)}, u32[]{:S(2)}, u32[]{:S(2)}) collective-permute-start(bf16[32,4096]{1,0:T(8,128)(2,1)S(1)} %get-tuple-element.32), channel_id=1, source_target_pairs={{0,2},{2,0},{4,6},{6,4},{8,10},{10,8},{12,14},{14,12},{16,18},{18,... | collective-permute-start | bytes 786440 | tf_op jit(solution)/shard_map/ppermute | solution.py:35
  190.0 11.5 %collective-permute-start.35 = (bf16[32,4096]{1,0:T(8,128)(2,1)S(1)}, bf16[32,4096]{1,0:T(8,128)(2,1)S(1)}, u32[]{:S(2)}, u32[]{:S(2)}) collective-permute-start(bf16[32,4096]{1,0:T(8,128)(2,1)S(1)} %get-tuple-element.33), channel_id=1, source_target_pairs={{0,4},{2,6},{4,0},{6,2},{8,12},{10,14},{12,8},{14,10},{16,20},{18,... | collective-permute-start | bytes 786440 | tf_op jit(solution)/shard_map/ppermute | solution.py:35
  200.2 15.1 %collective-permute-start.37 = (bf16[32,4096]{1,0:T(8,128)(2,1)S(1)}, bf16[32,4096]{1,0:T(8,128)(2,1)S(1)}, u32[]{:S(2)}, u32[]{:S(2)}) collective-permute-start(bf16[32,4096]{1,0:T(8,128)(2,1)S(1)} %get-tuple-element.34), channel_id=1, source_target_pairs={{0,2},{2,0},{4,6},{6,4},{8,10},{10,8},{12,14},{14,12},{16,18},{18,... | collective-permute-start | bytes 786440 | tf_op jit(solution)/shard_map/ppermute | solution.py:35
  200.8 14.6 %collective-permute-start.38 = (bf16[32,4096]{1,0:T(8,128)(2,1)S(1)}, bf16[32,4096]{1,0:T(8,128)(2,1)S(1)}, u32[]{:S(2)}, u32[]{:S(2)}) collective-permute-start(bf16[32,4096]{1,0:T(8,128)(2,1)S(1)} %get-tuple-element.35), channel_id=1, source_target_pairs={{0,4},{2,6},{4,0},{6,2},{8,12},{10,14},{12,8},{14,10},{16,20},{18,... | collective-permute-start | bytes 786440 | tf_op jit(solution)/shard_map/ppermute | solution.py:35
  201.8 13.6 %collective-permute-start.30 = (bf16[32,4096]{1,0:T(8,128)(2,1)S(1)}, bf16[32,4096]{1,0:T(8,128)(2,1)S(1)}, u32[]{:S(2)}, u32[]{:S(2)}) collective-permute-start(bf16[32,4096]{1,0:T(8,128)(2,1)S(1)} %get-tuple-element.43), channel_id=1, source_target_pairs={{0,24},{2,26},{4,28},{6,30},{8,0},{10,2},{12,4},{14,6},{16,8},{18,... | collective-permute-start | bytes 786440 | tf_op jit(solution)/shard_map/ppermute | solution.py:38
  206.0 10.7 %collective-permute-start.36 = (bf16[32,4096]{1,0:T(8,128)(2,1)S(1)}, bf16[32,4096]{1,0:T(8,128)(2,1)S(1)}, u32[]{:S(2)}, u32[]{:S(2)}) collective-permute-start(bf16[32,4096]{1,0:T(8,128)(2,1)S(1)} %get-tuple-element.44), channel_id=1, source_target_pairs={{0,8},{2,10},{4,12},{6,14},{8,16},{10,18},{12,20},{14,22},{16,24},... | collective-permute-start | bytes 786440 | tf_op jit(solution)/shard_map/ppermute | solution.py:38
  206.0 18.2 %collective-permute-start.33 = (bf16[32,4096]{1,0:T(8,128)(2,1)S(1)}, bf16[32,4096]{1,0:T(8,128)(2,1)S(1)}, u32[]{:S(2)}, u32[]{:S(2)}) collective-permute-start(bf16[32,4096]{1,0:T(8,128)(2,1)S(1)} %get-tuple-element.45), channel_id=1, source_target_pairs={{0,16},{2,18},{4,20},{6,22},{8,24},{10,26},{12,28},{14,30},{16,0},... | collective-permute-start | bytes 786440 | tf_op jit(solution)/shard_map/ppermute | solution.py:38
  (28 other events, 286.1 us)
